TPU v7x, 128 devices: a whole 4x4x4 slice. The times are simulated.
128 devices in a mesh: group: 8 (over y_hi, x), row: 16 (over z, y_lo, core).
Axes of the slice: x: 4, y: 4 (y_hi: 2, y_lo: 2; y = y_hi * 2 + y_lo), z: 4, core: 2. Of those that a mesh axis runs over, the one named last changes fastest.
Arguments:
- embeds: bfloat16 [65536, 768], P(('group', 'row')), may hold values from -120 to 120
- member: int32 [65536], P(('group', 'row')), may hold values from 0 to 7, as said below
Outputs:
- nearest: float32 [65536], P(('group', 'row'))
Inputs may be any that keep to these rules, and one draw needn't show every extreme that they name: `member`: rows come in aligned blocks of 512; no cluster takes more than 128 rows of one block. For each remainder of the block index modulo the row axis's size, one cluster takes exactly 128 rows of every block with that remainder.
All inputs are finite; a program needn't handle non-finite values.
Results may differ from a plain program's by a relative error of at most 0.00056.
Values may be sent and summed in bfloat16 or wider, within the bound.
No kernel may reach another device: no remote copies, remote signals or barrier semaphores. Data moves between devices by JAX's collectives and lax.ppermute only.
A program may use at most 128 MiB of HBM per device.

v0:
```python
import math

import jax
import jax.numpy as jnp
from jax import lax
from jax.sharding import PartitionSpec as P

absent = -4.0


def block_maxima(own_rows, own_flags, column_rows, column_flags, own_ids, column_ids):
    stride = math.gcd(column_rows.shape[0], 2048)
    number = column_rows.shape[0] // stride
    pieces = column_rows.reshape(number, stride, column_rows.shape[1])
    piece_flags = column_flags.reshape(number, stride)
    piece_ids = column_ids.reshape(number, stride)
    own_keep = own_flags > 0

    def visit(row_best, item):
        piece_rows, flags_part, ids_part = item
        scores = lax.dot_general(
            own_rows, piece_rows, (((1,), (1,)), ((), ())), preferred_element_type=jnp.float32
        )
        keep = (
            own_keep[:, None] & (flags_part[None, :] > 0) & (own_ids[:, None] != ids_part[None, :])
        )
        masked = jnp.where(keep, scores, absent)
        return (jnp.maximum(row_best, jnp.max(masked, axis=1)), jnp.max(masked, axis=0))

    start_best = jnp.full((own_rows.shape[0],), absent, jnp.float32)
    row_best, column_best = lax.scan(visit, start_best, (pieces, piece_flags, piece_ids))
    return (row_best, column_best.reshape(-1))


def on_device(embeds, member):
    groups = lax.axis_size("group")
    block_rows = embeds.shape[0]
    per_cluster = 2 * block_rows // groups
    capacity = groups * per_cluster
    values = embeds.astype(jnp.float32)
    normed = (values * lax.rsqrt(jnp.sum(values * values, axis=1, keepdims=True) + 1e-06)).astype(
        jnp.bfloat16
    )
    hits = (member[:, None] == jnp.arange(groups, dtype=jnp.int32)[None, :]).astype(jnp.int32)
    ranking = jnp.sum(jnp.cumsum(hits, axis=0) * hits, axis=1) - 1
    target = member * per_cluster + ranking
    placer = (jnp.arange(capacity, dtype=jnp.int32)[:, None] == target[None, :]).astype(
        jnp.bfloat16
    )
    outgoing = jnp.dot(placer, normed, preferred_element_type=jnp.float32).astype(jnp.bfloat16)
    counts = jnp.sum(hits, axis=0)
    filled = (jnp.arange(per_cluster, dtype=jnp.int32)[None, :] < counts[:, None]).astype(
        jnp.bfloat16
    )
    arrived, arrived_flags = (
        lax.all_to_all(
            outgoing.reshape(groups, per_cluster, -1),
            "group",
            split_axis=0,
            concat_axis=0,
            tiled=True,
        ),
        lax.all_to_all(filled, "group", split_axis=0, concat_axis=0, tiled=True),
    )
    own_rows = arrived.reshape(capacity, -1)
    own_flags = arrived_flags.reshape(capacity)
    own_ids = lax.axis_index("row") * capacity + jnp.arange(capacity, dtype=jnp.int32)
    initial = jnp.full((capacity,), absent, jnp.float32)
    column_rows = lax.all_gather(own_rows, "row", axis=0, tiled=True)
    column_flags = lax.all_gather(own_flags, "row", axis=0, tiled=True)
    column_ids = jnp.arange(column_rows.shape[0], dtype=jnp.int32)
    found, unused_columns = block_maxima(
        own_rows, own_flags, column_rows, column_flags, own_ids, column_ids
    )
    nearest = jnp.maximum(initial, found)
    homeward = lax.all_to_all(
        nearest.reshape(groups, per_cluster), "group", split_axis=0, concat_axis=0, tiled=True
    )
    return homeward.reshape(-1)[target]


def solution(mesh):
    in_specs = (P(("group", "row"), None), P(("group", "row")))
    out_specs = P(("group", "row"))
    return jax.shard_map(
        on_device, mesh=mesh, in_specs=in_specs, out_specs=out_specs, check_vma=False
    )
```

profile of v0, /device:TPU:1, one launch (start us, length us, event | category | flops | bytes accessed | tf_op | source)
XLA Modules:
  0.0 246.5 jit_solution(17565139092833224877)
XLA Ops:
  6.5 0.0 all-gather.2.cloned.1.call-start
  6.5 0.7 fusion.14
  7.2 1.1 reduce-window.6
  8.4 0.2 slice_reduce_fusion
  8.6 0.9 fusion.13
  9.5 0.7 compare_select_fusion
  10.2 1.4 fusion.8
  11.5 2.3 fusion.7
  13.8 29.3 %all_to_all.20 = bf16[8,128,768]{2,1,0:T(8,128)(2,1)} all-to-all(bf16[8,128,768]{2,1,0:T(8,128)(2,1)S(1)} %bitcast.34), channel_id=1, replica_groups=mesh['group'=8,'row'=16] {'group'}, dimensions={0} | all-to-all | bytes 3145728 | tf_op jit(solution)/shard_map/all_to_all | solution.py:56
  43.2 0.0 all-gather.2.cloned.1.call-update
  43.2 0.7 compare_convert_fusion
  43.9 3.3 %all-to-all-start = ((bf16[8,1,128]{2,1,0:T(2,128)(2,1)}), bf16[8,1,128]{2,1,0:T(2,128)(2,1)S(1)}, u32[]{:S(2)}, u32[]{:S(2)}) async-start(bf16[8,1,128]{2,1,0:T(2,128)(2,1)} %compare_convert_fusion), calls=%async_computation | async-start | bytes 8192 | tf_op jit(solution)/shard_map/all_to_all | solution.py:63
  47.2 6.4 %all-to-all-done = bf16[8,1,128]{2,1,0:T(2,128)(2,1)S(1)} async-done(((bf16[8,1,128]{2,1,0:T(2,128)(2,1)}), bf16[8,1,128]{2,1,0:T(2,128)(2,1)S(1)}, u32[]{:S(2)}, u32[]{:S(2)}) %all-to-all-start) | async-done | bytes 2080 | tf_op jit(solution)/shard_map/all_to_all | solution.py:63
  53.6 23.1 %all_gather.6 = bf16[16384]{0:T(1024)(128)(2,1)S(1)} all-gather(bf16[1024]{0:T(1024)(128)(2,1)S(1)} %bitcast.37), channel_id=1, replica_groups=mesh['group'=8,'row'=16] {'row'}, dimensions={0}, use_global_device_ids=true | all-gather | bytes 34816 | tf_op jit(solution)/shard_map/all_gather | solution.py:70
  76.8 97.7 %all-gather.2.cloned.1.call-done = bf16[16384,768]{1,0:T(8,128)(2,1)} async-done(((bf16[1024,768]{1,0:T(8,128)(2,1)}), bf16[16384,768]{1,0:T(8,128)(2,1)}) %all-gather.2.cloned.1.call-update) | async-done | bytes 25165840 | tf_op jit(solution)/shard_map/all_gather | solution.py:69
  174.5 48.2 %while.11 = (s32[]{:T(128)}, f32[1024]{0:T(1024)S(1)}, pred[1024]{0:T(1024)(128)(4,1)S(1)}, bf16[8,2048]{1,0:T(8,128)(2,1)S(1)}, s32[8,2048]{1,0:T(8,128)S(1)}, ...) while((s32[]{:T(128)}, f32[1024]{0:T(1024)S(1)}, ...), condition=%wide.region_7.8_spmd.clone, body=%wide.region_5.7_spmd.clone.sunk | while | flops 3231719424 | bytes 4777595 | solution.py:31
  174.5 5.9 %fusion.21 = f32[1024]{0:T(1024)S(1)} fusion(bf16[1024,768]{1,0:T(8,128)(2,1)} %get-tuple-element.173, s32[1024]{0:T(1024)S(1)} %iota_add_fusion.2, s32[2048]{0:T(1024)S(1)} %bitcast.35, pred[1024]{0:T(1024)(128)(4,1)S(1)} %get-tuple-element.169, pred[2048]{0:T(1024)(128)(4,1)S(1)} %compare_reduce_fusion.2, ...), kind=kOutput, calls=%fused_computation.3.clone.1 | convolution fusion | flops 3231710208 | bytes 4738560 | tf_op jit(solution)/shard_map/while/body/eval_jaxpr/dot_general | solution.py:21
  180.6 5.9 %fusion.21 = f32[1024]{0:T(1024)S(1)} fusion(bf16[1024,768]{1,0:T(8,128)(2,1)} %get-tuple-element.173, s32[1024]{0:T(1024)S(1)} %iota_add_fusion.2, s32[2048]{0:T(1024)S(1)} %bitcast.35, pred[1024]{0:T(1024)(128)(4,1)S(1)} %get-tuple-element.169, pred[2048]{0:T(1024)(128)(4,1)S(1)} %compare_reduce_fusion.2, ...), kind=kOutput, calls=%fused_computation.3.clone.1 | convolution fusion | flops 3231710208 | bytes 4738560 | tf_op jit(solution)/shard_map/while/body/eval_jaxpr/dot_general | solution.py:21
  186.6 5.9 %fusion.21 = f32[1024]{0:T(1024)S(1)} fusion(bf16[1024,768]{1,0:T(8,128)(2,1)} %get-tuple-element.173, s32[1024]{0:T(1024)S(1)} %iota_add_fusion.2, s32[2048]{0:T(1024)S(1)} %bitcast.35, pred[1024]{0:T(1024)(128)(4,1)S(1)} %get-tuple-element.169, pred[2048]{0:T(1024)(128)(4,1)S(1)} %compare_reduce_fusion.2, ...), kind=kOutput, calls=%fused_computation.3.clone.1 | convolution fusion | flops 3231710208 | bytes 4738560 | tf_op jit(solution)/shard_map/while/body/eval_jaxpr/dot_general | solution.py:21
  192.6 5.9 %fusion.21 = f32[1024]{0:T(1024)S(1)} fusion(bf16[1024,768]{1,0:T(8,128)(2,1)} %get-tuple-element.173, s32[1024]{0:T(1024)S(1)} %iota_add_fusion.2, s32[2048]{0:T(1024)S(1)} %bitcast.35, pred[1024]{0:T(1024)(128)(4,1)S(1)} %get-tuple-element.169, pred[2048]{0:T(1024)(128)(4,1)S(1)} %compare_reduce_fusion.2, ...), kind=kOutput, calls=%fused_computation.3.clone.1 | convolution fusion | flops 3231710208 | bytes 4738560 | tf_op jit(solution)/shard_map/while/body/eval_jaxpr/dot_general | solution.py:21
  198.7 5.9 %fusion.21 = f32[1024]{0:T(1024)S(1)} fusion(bf16[1024,768]{1,0:T(8,128)(2,1)} %get-tuple-element.173, s32[1024]{0:T(1024)S(1)} %iota_add_fusion.2, s32[2048]{0:T(1024)S(1)} %bitcast.35, pred[1024]{0:T(1024)(128)(4,1)S(1)} %get-tuple-element.169, pred[2048]{0:T(1024)(128)(4,1)S(1)} %compare_reduce_fusion.2, ...), kind=kOutput, calls=%fused_computation.3.clone.1 | convolution fusion | flops 3231710208 | bytes 4738560 | tf_op jit(solution)/shard_map/while/body/eval_jaxpr/dot_general | solution.py:21
  204.7 5.9 %fusion.21 = f32[1024]{0:T(1024)S(1)} fusion(bf16[1024,768]{1,0:T(8,128)(2,1)} %get-tuple-element.173, s32[1024]{0:T(1024)S(1)} %iota_add_fusion.2, s32[2048]{0:T(1024)S(1)} %bitcast.35, pred[1024]{0:T(1024)(128)(4,1)S(1)} %get-tuple-element.169, pred[2048]{0:T(1024)(128)(4,1)S(1)} %compare_reduce_fusion.2, ...), kind=kOutput, calls=%fused_computation.3.clone.1 | convolution fusion | flops 3231710208 | bytes 4738560 | tf_op jit(solution)/shard_map/while/body/eval_jaxpr/dot_general | solution.py:21
  210.7 5.9 %fusion.21 = f32[1024]{0:T(1024)S(1)} fusion(bf16[1024,768]{1,0:T(8,128)(2,1)} %get-tuple-element.173, s32[1024]{0:T(1024)S(1)} %iota_add_fusion.2, s32[2048]{0:T(1024)S(1)} %bitcast.35, pred[1024]{0:T(1024)(128)(4,1)S(1)} %get-tuple-element.169, pred[2048]{0:T(1024)(128)(4,1)S(1)} %compare_reduce_fusion.2, ...), kind=kOutput, calls=%fused_computation.3.clone.1 | convolution fusion | flops 3231710208 | bytes 4738560 | tf_op jit(solution)/shard_map/while/body/eval_jaxpr/dot_general | solution.py:21
  216.8 5.9 %fusion.21 = f32[1024]{0:T(1024)S(1)} fusion(bf16[1024,768]{1,0:T(8,128)(2,1)} %get-tuple-element.173, s32[1024]{0:T(1024)S(1)} %iota_add_fusion.2, s32[2048]{0:T(1024)S(1)} %bitcast.35, pred[1024]{0:T(1024)(128)(4,1)S(1)} %get-tuple-element.169, pred[2048]{0:T(1024)(128)(4,1)S(1)} %compare_reduce_fusion.2, ...), kind=kOutput, calls=%fused_computation.3.clone.1 | convolution fusion | flops 3231710208 | bytes 4738560 | tf_op jit(solution)/shard_map/while/body/eval_jaxpr/dot_general | solution.py:21
  222.7 0.6 broadcast_maximum_fusion
  223.3 6.4 %all-to-all-start.2 = ((f32[8,1,128]{2,1,0:T(1,128)}), f32[8,1,128]{2,1,0:T(1,128)S(1)}, u32[]{:S(2)}, u32[]{:S(2)}) async-start(f32[8,1,128]{2,1,0:T(1,128)} %bitcast.6), calls=%async_computation.2 | async-start | bytes 8192 | tf_op jit(solution)/shard_map/all_to_all | solution.py:76
  229.7 6.5 %all-to-all-done.2 = f32[8,1,128]{2,1,0:T(1,128)S(1)} async-done(((f32[8,1,128]{2,1,0:T(1,128)}), f32[8,1,128]{2,1,0:T(1,128)S(1)}, u32[]{:S(2)}, u32[]{:S(2)}) %all-to-all-start.2) | async-done | bytes 4128 | tf_op jit(solution)/shard_map/all_to_all | solution.py:76
  236.2 3.4 %gather_fusion = f32[512]{0:T(512)} fusion(f32[1024]{0:T(1024)S(1)} %bitcast.31, s32[1024]{0:T(1024)S(1)} %pad_clamp_fusion), kind=kCustom, calls=%fused_computation | custom fusion | bytes 6144 | tf_op jit(solution)/shard_map/gather | solution.py:79
  (41 shorter events, 0.7 us)
Async XLA Ops:
  6.5 167.9 %all-gather.2.cloned.1.call-start = ((), (), s32[]{:S(2)}) async-start(), calls=%async_computation.3 | async-start | bytes 26738688 | tf_op jit(solution)/shard_map/all_gather | solution.py:69
  43.9 9.7 %all-to-all-start = ((bf16[8,1,128]{2,1,0:T(2,128)(2,1)}), bf16[8,1,128]{2,1,0:T(2,128)(2,1)S(1)}, u32[]{:S(2)}, u32[]{:S(2)}) async-start(bf16[8,1,128]{2,1,0:T(2,128)(2,1)} %compare_convert_fusion), calls=%async_computation | async-start | bytes 8192 | tf_op jit(solution)/shard_map/all_to_all | solution.py:63
  223.3 12.9 %all-to-all-start.2 = ((f32[8,1,128]{2,1,0:T(1,128)}), f32[8,1,128]{2,1,0:T(1,128)S(1)}, u32[]{:S(2)}, u32[]{:S(2)}) async-start(f32[8,1,128]{2,1,0:T(1,128)} %bitcast.6), calls=%async_computation.2 | async-start | bytes 8192 | tf_op jit(solution)/shard_map/all_to_all | solution.py:76
Sparse Core Ops, SparseCore 0:
  43.3 131.1 all-gather.1
where the time goes:
time: 247 us; the launch traced here: 246 us
  waiting for transfers between devices  111 us (45%)
  blocking collectives  52.5 us (21%)
  matrix products  49.6 us (20%)
  between operations  13.5 us (5%)
  starting transfers between devices  9.69 us (4%)
  other arithmetic  6.56 us (3%)
  local copies, waits for them, and re-layouts  3.74 us (2%)
    all_gather x1, waiting for transfers between devices, on_device(): column_rows = lax.all_gather(own_rows, 'row', axis=0, tiled=True)  97.7 us
    dot_general x8, matrix products, visit(): lax.dot_general(own_rows, piece_rows, (((1,), (1,)), ((), ())), preferred...  47.3 us
    all_to_all x1, blocking collectives, on_device(): lax.all_to_all(outgoing.reshape(groups, per_cluster, -1), 'group', split_...  29.3 us
    all_gather x1, blocking collectives, on_device(): column_flags = lax.all_gather(own_flags, 'row', axis=0, tiled=True)  23.1 us
    all_to_all x1, waiting for transfers between devices, on_device(): lax.all_to_all(nearest.reshape(groups, per_cluster), 'group', split_axis=...  6.5 us
    all_to_all x1, starting transfers between devices, on_device(): lax.all_to_all(nearest.reshape(groups, per_cluster), 'group', split_axis=...  6.42 us
    all_to_all x1, waiting for transfers between devices, on_device(): lax.all_to_all(filled, 'group', split_axis=0, concat_axis=0, tiled=True)  6.41 us
  transfers between devices with their start and end apart: 3, of which 3 were waited for; matrix products, arithmetic and copies ran while one was open for 0% of the time, Pallas kernels for 0%

commit v1 on v0

v1 whole, which is shorter than its diff:
```python
import functools

import jax
import jax.numpy as jnp
from jax import lax
from jax.experimental import pallas as pl
from jax.experimental.pallas import tpu as pltpu
from jax.sharding import PartitionSpec as P

D = 768
RB = 512
GROUPS = 8
MOST = 128
META = 16
SENT = RB + META
HELD = 640
SHORT, LONG = 80, 144
TILE = 256
ABSENT = -4.0
LOW = -1e30
AXES = ("group", "row")

UNIT = ((1, 0, 0), (0, 1, 0), (0, 0, 1), (3, 0, 0), (0, 3, 0), (0, 0, 3))
PARENT = (None,) + (0, 0, 0, 2, 3, 1, 4, 5, 5, 6, 6, 4)
DIRS = (
    (None,) + (0, 1, 3, 5, 2, 4, 3, 4, 1, 0, 5, 1),
    (None,) + (2, 5, 4, 1, 0, 3, 0, 2, 5, 2, 4, 3),
)
SLOTS = len(PARENT)
FLIPPED = 10


def offsets():
    table = []
    for core in range(2):
        held = [(0, 0, 0)]
        for i in range(1, SLOTS):
            step, base = UNIT[DIRS[core][i]], held[PARENT[i]]
            held.append(tuple((a + b) % 4 for a, b in zip(step, base)))
        table.append(held)
    return table


def place(x, y, z, core):
    group = (y // 2) * 4 + x
    row = (z * 2 + y % 2) * 2 + core
    return group * 16 + row


def fetch(block, steps):
    pairs = []
    for x in range(4):
        for y in range(4):
            for z in range(4):
                for core in range(2):
                    dx, dy, dz = steps[core]
                    source = place((x + dx) % 4, (y + dy) % 4, (z + dz) % 4, core)
                    pairs.append((source, place(x, y, z, core)))
    return lax.ppermute(block, AXES, sorted(pairs))


def flip(block):
    return lax.ppermute(block, AXES, [(i, i ^ 1) for i in range(128)])


def prepare_kernel(embeds_ref, member_ref, block_ref, target_ref):
    member = member_ref[...].astype(jnp.float32)
    column = jnp.transpose(jnp.broadcast_to(member, (128, RB)))[:, 0:1]
    above = lax.broadcasted_iota(jnp.int32, (RB, RB), 0)
    across = lax.broadcasted_iota(jnp.int32, (RB, RB), 1)
    before = (column < member) | ((column == member) & (above < across))
    target = jnp.sum(before.astype(jnp.float32), axis=0, keepdims=True).astype(jnp.int32)
    target_ref[...] = target
    values = embeds_ref[...].astype(jnp.float32)
    total = jnp.sum(values * values, axis=1, keepdims=True)
    normed = (values * lax.rsqrt(total + 1e-06)).astype(jnp.bfloat16)
    placer = (above == target).astype(jnp.bfloat16)
    block_ref[0:RB, :] = jnp.dot(placer, normed, preferred_element_type=jnp.float32).astype(
        jnp.bfloat16
    )
    lane = lax.broadcasted_iota(jnp.int32, (RB, D), 1).astype(jnp.float32)
    counts = jnp.sum((column == lane).astype(jnp.float32), axis=0, keepdims=True)
    block_ref[RB:SENT, :] = jnp.broadcast_to(counts, (META, D)).astype(jnp.bfloat16)


def prepare(embeds, member):
    return pl.pallas_call(
        prepare_kernel,
        out_shape=(
            jax.ShapeDtypeStruct((SENT, D), jnp.bfloat16),
            jax.ShapeDtypeStruct((1, RB), jnp.int32),
        ),
        name="prepare",
    )(embeds, member.reshape(1, RB))


def gram_kernel(new, total, *refs):
    blocks = refs[:total]
    out_ref = refs[total]
    (held, rows, bias, best, kept, counts_v, counts_s, start_s, put_s, sems, meta_sem) = refs[
        total + 1 :
    ]
    copies = []
    for k in range(total):
        copy = pltpu.make_async_copy(blocks[k], held.at[k, pl.ds(0, SENT)], sems.at[k])
        copy.start()
        copies.append(copy)
    rows[...] = jnp.zeros_like(rows)
    for k in range(total):
        held[k, SENT:HELD, :] = jnp.zeros((HELD - SENT, D), jnp.bfloat16)
        kept[k] = jnp.full((HELD, 128), LOW, jnp.float32)
        start_s[k] = 0
    for k in range(total):
        copies[k].wait()
        counts_v[k : k + 1, :] = held[k, RB:SENT, 0:128].astype(jnp.float32)[0:1].astype(jnp.int32)
    fetch_counts = pltpu.make_async_copy(counts_v, counts_s, meta_sem)
    fetch_counts.start()
    fetch_counts.wait()

    def bias_of(length, first, low, high):
        at = first + lax.broadcasted_iota(jnp.int32, (length, 128), 0)
        return jnp.where((at >= low) & (at < high), 0.0, LOW)

    def one_cluster(c, carry):
        put = jnp.int32(0)
        new_rows = jnp.int32(0)
        for k in range(total):
            low = start_s[k]
            high = low + counts_s[k, c]
            first = pl.multiple_of((low // 16) * 16, 16)
            tiles = jnp.where(high > low, (high - first + 15) // 16, 0)
            put = pl.multiple_of(put, 16)
            put_s[k] = put

            @pl.when(tiles > 0)
            def _(k=k, low=low, high=high, first=first, put=put):
                rows[pl.ds(put, SHORT), :] = held[k, pl.ds(first, SHORT), :]
                bias[pl.ds(put, SHORT), :] = bias_of(SHORT, first, low, high)

            @pl.when(tiles > SHORT // 16)
            def _(k=k, low=low, high=high, first=first, put=put):
                more = pl.multiple_of(put + SHORT, 16)
                rest = pl.multiple_of(first + SHORT, 16)
                rows[pl.ds(more, LONG - SHORT), :] = held[k, pl.ds(rest, LONG - SHORT), :]
                bias[pl.ds(more, LONG - SHORT), :] = bias_of(LONG - SHORT, rest, low, high)

            put = put + tiles * 16
            if k == new - 1:
                new_rows = put
        put = pl.multiple_of(put, 16)
        bias[pl.ds(put, TILE), :] = jnp.full((TILE, 128), LOW, jnp.float32)
        column_tiles = (new_rows + TILE - 1) // TILE
        row_tiles = (put + TILE - 1) // TILE

        def clear(m, carry):
            best[pl.ds(pl.multiple_of(m * TILE, TILE), TILE), :] = jnp.full(
                (TILE, 128), LOW, jnp.float32
            )
            return carry

        lax.fori_loop(0, row_tiles, clear, 0)

        def one_column_tile(n, carry):
            here = pl.multiple_of(n * TILE, TILE)
            columns = rows[pl.ds(here, TILE), :]
            column_bias = jnp.transpose(bias[pl.ds(here, TILE), :])[0:1, :]

            def visit(scores, at, column_best):
                masked = scores + column_bias
                best[pl.ds(at, TILE), :] = jnp.maximum(
                    best[pl.ds(at, TILE), :],
                    jnp.maximum(masked[:, :128], masked[:, 128:]),
                )
                row_bias = bias[pl.ds(at, TILE), :]
                masked = scores + jnp.concatenate([row_bias, row_bias], axis=1)
                return jnp.maximum(column_best, jnp.max(masked.reshape(TILE // 8, 8, TILE), axis=0))

            def scores_at(at):
                return lax.dot_general(
                    rows[pl.ds(at, TILE), :],
                    columns,
                    (((1,), (1,)), ((), ())),
                    preferred_element_type=jnp.float32,
                )

            same = lax.broadcasted_iota(jnp.int32, (TILE, TILE), 0) == lax.broadcasted_iota(
                jnp.int32, (TILE, TILE), 1
            )
            column_best = jnp.full((8, TILE), LOW, jnp.float32)
            column_best = visit(jnp.where(same, LOW, scores_at(here)), here, column_best)

            def one_row_tile(m, column_best):
                at = pl.multiple_of(m * TILE, TILE)
                return visit(scores_at(at), at, column_best)

            column_best = lax.fori_loop(n + 1, row_tiles, one_row_tile, column_best)
            top = jnp.max(column_best, axis=0, keepdims=True)
            down = jnp.transpose(jnp.broadcast_to(top, (128, TILE)))
            best[pl.ds(here, TILE), :] = jnp.maximum(best[pl.ds(here, TILE), :], down)
            return carry

        lax.fori_loop(0, column_tiles, one_column_tile, 0)

        for k in range(total):
            low = start_s[k]
            high = low + counts_s[k, c]
            first = pl.multiple_of((low // 16) * 16, 16)
            tiles = jnp.where(high > low, (high - first + 15) // 16, 0)
            put = pl.multiple_of(put_s[k], 16)

            def keep(k, first, put, length):
                kept[k, pl.ds(first, length), :] = jnp.maximum(
                    kept[k, pl.ds(first, length), :],
                    best[pl.ds(put, length), :] + bias_of(length, first, low, high),
                )

            @pl.when(tiles > 0)
            def _(k=k, low=low, high=high, first=first, put=put):
                kept[k, pl.ds(first, SHORT), :] = jnp.maximum(
                    kept[k, pl.ds(first, SHORT), :],
                    best[pl.ds(put, SHORT), :] + bias_of(SHORT, first, low, high),
                )

            @pl.when(tiles > SHORT // 16)
            def _(k=k, low=low, high=high, first=first, put=put):
                more = pl.multiple_of(put + SHORT, 16)
                rest = pl.multiple_of(first + SHORT, 16)
                kept[k, pl.ds(rest, LONG - SHORT), :] = jnp.maximum(
                    kept[k, pl.ds(rest, LONG - SHORT), :],
                    best[pl.ds(more, LONG - SHORT), :] + bias_of(LONG - SHORT, rest, low, high),
                )

            start_s[k] = high
        return carry

    lax.fori_loop(0, GROUPS, one_cluster, 0)
    for k in range(total):
        turned = jnp.transpose(kept[k, 0:RB, :])
        out_ref[k : k + 1, :] = jnp.max(turned, axis=0, keepdims=True)


def gram(new_blocks, old_blocks):
    new, total = len(new_blocks), len(new_blocks) + len(old_blocks)
    deep = -(-(total * LONG) // TILE) * TILE + TILE
    return pl.pallas_call(
        functools.partial(gram_kernel, new, total),
        out_shape=jax.ShapeDtypeStruct((total, RB), jnp.float32),
        in_specs=[pl.BlockSpec(memory_space=pl.ANY)] * total,
        scratch_shapes=[
            pltpu.VMEM((total, HELD, D), jnp.bfloat16),
            pltpu.VMEM((deep, D), jnp.bfloat16),
            pltpu.VMEM((deep, 128), jnp.float32),
            pltpu.VMEM((deep, 128), jnp.float32),
            pltpu.VMEM((total, HELD, 128), jnp.float32),
            pltpu.VMEM((total, 128), jnp.int32),
            pltpu.SMEM((total, 128), jnp.int32),
            pltpu.SMEM((total,), jnp.int32),
            pltpu.SMEM((total,), jnp.int32),
            pltpu.SemaphoreType.DMA((total,)),
            pltpu.SemaphoreType.DMA,
        ],
        compiler_params=pltpu.CompilerParams(vmem_limit_bytes=56 * 2**20),
        cost_estimate=pl.CostEstimate(
            flops=2 * 8 * 70 * 70 * D * new * total, bytes_accessed=total * SENT * D * 2, transcendentals=0
        ),
        name=f"gram_{new}_{total}",
    )(*new_blocks, *old_blocks)


def scatter_kernel(found_ref, where_ref, out_ref):
    out_ref[...] = jnp.full_like(out_ref, ABSENT)
    for k in range(found_ref.shape[0]):
        out_ref[pl.ds(where_ref[k], 1), :] = jnp.maximum(found_ref[k : k + 1, :], ABSENT)


def scatter(found, where):
    return pl.pallas_call(
        scatter_kernel,
        out_shape=jax.ShapeDtypeStruct((128, RB), jnp.float32),
        in_specs=[pl.BlockSpec(memory_space=pltpu.VMEM), pl.BlockSpec(memory_space=pltpu.SMEM)],
        out_specs=pl.BlockSpec(memory_space=pltpu.VMEM),
        name="scatter",
    )(found, where)


def finish_kernel(arrived_ref, target_ref, out_ref):
    best = jnp.max(arrived_ref[...], axis=0, keepdims=True)
    column = jnp.transpose(jnp.broadcast_to(best, (128, RB)))[:, 0:1]
    above = lax.broadcasted_iota(jnp.int32, (RB, RB), 0)
    picked = jnp.where(above == target_ref[...], column, LOW)
    out_ref[...] = jnp.max(picked, axis=0, keepdims=True)


def finish(arrived, target):
    return pl.pallas_call(
        finish_kernel, out_shape=jax.ShapeDtypeStruct((1, RB), jnp.float32), name="finish"
    )(arrived, target)


def homes():
    group, row = lax.axis_index("group"), lax.axis_index("row")
    x, y, z, core = group % 4, (group // 4) * 2 + (row // 2) % 2, row // 4, row % 2
    table = jnp.array(offsets(), jnp.int32)
    own = jnp.where(core == 0, table[0], table[1])
    other = jnp.where(core == 0, table[1], table[0])[:FLIPPED]
    cores = jnp.concatenate([jnp.full((SLOTS,), core), jnp.full((FLIPPED,), 1 - core)])
    steps = jnp.concatenate([own, other])
    return place((x + steps[:, 0]) % 4, (y + steps[:, 1]) % 4, (z + steps[:, 2]) % 4, cores).astype(
        jnp.int32
    )


def on_device(embeds, member):
    block, target = prepare(embeds, member)
    held = [block]
    for i in range(1, SLOTS):
        held.append(fetch(held[PARENT[i]], (UNIT[DIRS[0][i]], UNIT[DIRS[1][i]])))
    flipped = [flip(held[i]) for i in range(FLIPPED)]
    found = gram(held, flipped)
    outgoing = scatter(found, homes())
    arrived = lax.all_to_all(outgoing, AXES, split_axis=0, concat_axis=0, tiled=True)
    return finish(arrived, target).reshape(-1)


def solution(mesh):
    in_specs = (P(AXES, None), P(AXES))
    return jax.shard_map(
        on_device, mesh=mesh, in_specs=in_specs, out_specs=P(AXES), check_vma=False
    )
```

time: 247 us -> 189 us (0.77)
  Pallas kernels: 0 us -> 97.8 us
  waiting for transfers between devices: 111 us -> 26.6 us
  matrix products: 49.6 us -> 0 us
  blocking collectives: 52.5 us -> 20 us
  starting transfers between devices: 9.69 us -> 39.5 us
  between operations: 13.5 us -> 0.18 us
  other arithmetic: 6.56 us -> 0.62 us
    pallas_call x0 -> x4, Pallas kernels: none -> 97.8 us  [the longest x1 91.2 us: gram(): pl.pallas_call(functools.partial(gram_kernel, new, total), out_shape=jax....]
    all_gather x1 -> x0, waiting for transfers between devices: 97.7 us -> none  [on_device(): column_rows = lax.all_gather(own_rows, 'row', axis=0, tiled=True)]
    dot_general x9 -> x0, matrix products: 49.6 us -> none  [the longest x8 47.3 us: visit(): lax.dot_general(own_rows, piece_rows, (((1,), (1,)), ((), ())), preferred...]
    ppermute x0 -> x22, starting transfers between devices: none -> 39.5 us  [the longest x10 21.9 us: flip(): return lax.ppermute(block, AXES, [(i, i ^ 1) for i in range(128)])]
    ppermute x0 -> x22, waiting for transfers between devices: none -> 26.6 us  [the longest x12 25.5 us: fetch(): return lax.ppermute(block, AXES, sorted(pairs))]
    all_gather x1 -> x0, blocking collectives: 23.1 us -> none  [on_device(): column_flags = lax.all_gather(own_flags, 'row', axis=0, tiled=True)]
    all_to_all x2 -> x0, waiting for transfers between devices: 12.9 us -> none  [the longest x1 6.5 us: on_device(): lax.all_to_all(nearest.reshape(groups, per_cluster), 'group', split_axis=...]
    all_to_all x2 -> x0, starting transfers between devices: 9.68 us -> none  [the longest x1 6.42 us: on_device(): lax.all_to_all(nearest.reshape(groups, per_cluster), 'group', split_axis=...]
  transfers between devices with their start and end apart: 3 -> 22, of which waited for: 3 -> 6; matrix products, arithmetic and copies ran while one was open for 0% -> 0% of each run, Pallas kernels for 0% -> 0%
where the time goes in v1:
time: 189 us; the launch traced here: 188 us
  Pallas kernels  97.8 us (52%)
  starting transfers between devices  39.5 us (21%)
  waiting for transfers between devices  26.6 us (14%)
  blocking collectives  20 us (11%)
  local copies, waits for them, and re-layouts  3.2 us (2%)
    pallas_call x1, Pallas kernels, gram(): pl.pallas_call(functools.partial(gram_kernel, new, total), out_shape=jax....  91.2 us
    ppermute x12, waiting for transfers between devices, fetch(): return lax.ppermute(block, AXES, sorted(pairs))  25.5 us
    ppermute x10, starting transfers between devices, flip(): return lax.ppermute(block, AXES, [(i, i ^ 1) for i in range(128)])  21.9 us
    all_to_all x1, blocking collectives, on_device(): lax.all_to_all(outgoing, AXES, split_axis=0, concat_axis=0, tiled=True)  20 us
    ppermute x12, starting transfers between devices, fetch(): return lax.ppermute(block, AXES, sorted(pairs))  17.6 us
  transfers between devices with their start and end apart: 22, of which 6 were waited for; matrix products, arithmetic and copies ran while one was open for 0% of the time, Pallas kernels for 0%

profile of v1, /device:TPU:1, one launch (start us, length us, event | category | flops | bytes accessed | tf_op | source)
XLA Modules:
  0.0 187.8 jit_solution(36772192314528084)
XLA Ops:
  0.0 3.2 %prepare.1 = (bf16[528,768]{1,0:T(8,128)(2,1)}, s32[1,512]{1,0:T(1,128)}) custom-call(bf16[512,768]{1,0:T(8,128)(2,1)} %embeds_ref.1, s32[1,512]{1,0:T(1,128)} %bitcast.24), custom_call_target="tpu_custom_call" | custom-call | tf_op jit(solution)/shard_map/prepare/pallas_call | solution.py:87
  3.2 2.5 %collective-permute-start.1 = (bf16[528,768]{1,0:T(8,128)(2,1)}, bf16[528,768]{1,0:T(8,128)(2,1)S(1)}, u32[]{:S(2)}, u32[]{:S(2)}) collective-permute-start(bf16[528,768]{1,0:T(8,128)(2,1)} %get-tuple-element.7.refs_0_), channel_id=1, source_target_pairs={{0,66},{1,5},{2,0},{3,7},{4,70},{5,9},{6,4},{7,11},{8,74},{9,13},{... | collective-permute-start | bytes 2433032 | tf_op jit(solution)/shard_map/ppermute | solution.py:59
  5.7 1.3 collective-permute-start.2
  7.0 2.1 %collective-permute-start = (bf16[528,768]{1,0:T(8,128)(2,1)}, bf16[528,768]{1,0:T(8,128)(2,1)S(1)}, u32[]{:S(2)}, u32[]{:S(2)}) collective-permute-start(bf16[528,768]{1,0:T(8,128)(2,1)} %get-tuple-element.7.refs_0_), channel_id=1, source_target_pairs={{0,48},{1,13},{2,50},{3,15},{4,52},{5,1},{6,54},{7,3},{8,56},{9,5}... | collective-permute-start | bytes 2433032 | tf_op jit(solution)/shard_map/ppermute | solution.py:59
  9.1 1.9 collective-permute-start.12
  10.9 7.0 %collective-permute-done.1.refs_2_ = bf16[528,768]{1,0:T(8,128)(2,1)S(1)} collective-permute-done((bf16[528,768]{1,0:T(8,128)(2,1)}, bf16[528,768]{1,0:T(8,128)(2,1)S(1)}, u32[]{:S(2)}, u32[]{:S(2)}) %collective-permute-start.1) | collective-permute-done | bytes 811040 | tf_op jit(solution)/shard_map/ppermute | solution.py:59
  17.9 2.7 %collective-permute-start.3 = (bf16[528,768]{1,0:T(8,128)(2,1)S(1)}, bf16[528,768]{1,0:T(8,128)(2,1)S(1)}, u32[]{:S(2)}, u32[]{:S(2)}) collective-permute-start(bf16[528,768]{1,0:T(8,128)(2,1)S(1)} %collective-permute-done.1.refs_2_), channel_id=1, source_target_pairs={{0,4},{1,67},{2,6},{3,1},{4,8},{5,71},{6,10},{7,5},{8,12},{9,75},{... | collective-permute-start | bytes 2433032 | tf_op jit(solution)/shard_map/ppermute | solution.py:59
  20.7 0.0 collective-permute-done.2.refs_3_
  20.7 2.5 %collective-permute-start.4 = (bf16[528,768]{1,0:T(8,128)(2,1)S(1)}, bf16[528,768]{1,0:T(8,128)(2,1)S(1)}, u32[]{:S(2)}, u32[]{:S(2)}) collective-permute-start(bf16[528,768]{1,0:T(8,128)(2,1)S(1)} %collective-permute-done.2.refs_3_), channel_id=1, source_target_pairs={{0,12},{1,49},{2,14},{3,51},{4,0},{5,53},{6,2},{7,55},{8,4},{9,57}... | collective-permute-start | bytes 2433032 | tf_op jit(solution)/shard_map/ppermute | solution.py:59
  23.1 0.0 collective-permute-done.refs_1_
  23.1 0.0 collective-permute-start.5
  23.2 2.4 %collective-permute-start.13 = (bf16[528,768]{1,0:T(8,128)(2,1)S(1)}, bf16[528,768]{1,0:T(8,128)(2,1)S(1)}, u32[]{:S(2)}, u32[]{:S(2)}) collective-permute-start(bf16[528,768]{1,0:T(8,128)(2,1)S(1)} %collective-permute-done.refs_1_), channel_id=1, source_target_pairs={{0,1},{1,0},{2,3},{3,2},{4,5},{5,4},{6,7},{7,6},{8,9},{9,8},{10,11... | collective-permute-start | bytes 2433032 | tf_op jit(solution)/shard_map/ppermute | solution.py:63
  25.5 0.0 collective-permute-done.12.refs_13_
  25.5 0.1 collective-permute-start.14
  25.6 4.2 %collective-permute-done.3.refs_4_ = bf16[528,768]{1,0:T(8,128)(2,1)S(1)} collective-permute-done((bf16[528,768]{1,0:T(8,128)(2,1)S(1)}, bf16[528,768]{1,0:T(8,128)(2,1)S(1)}, u32[]{:S(2)}, u32[]{:S(2)}) %collective-permute-start.3) | collective-permute-done | bytes 811040 | tf_op jit(solution)/shard_map/ppermute | solution.py:59
  29.9 2.2 %collective-permute-start.15 = (bf16[528,768]{1,0:T(8,128)(2,1)S(1)}, bf16[528,768]{1,0:T(8,128)(2,1)S(1)}, u32[]{:S(2)}, u32[]{:S(2)}) collective-permute-start(bf16[528,768]{1,0:T(8,128)(2,1)S(1)} %collective-permute-done.2.refs_3_), channel_id=1, source_target_pairs={{0,1},{1,0},{2,3},{3,2},{4,5},{5,4},{6,7},{7,6},{8,9},{9,8},{10,11... | collective-permute-start | bytes 2433032 | tf_op jit(solution)/shard_map/ppermute | solution.py:63
  32.1 0.3 collective-permute-done.4.refs_5_
  32.3 3.5 %collective-permute-start.6 = (bf16[528,768]{1,0:T(8,128)(2,1)S(1)}, bf16[528,768]{1,0:T(8,128)(2,1)}, u32[]{:S(2)}, u32[]{:S(2)}) collective-permute-start(bf16[528,768]{1,0:T(8,128)(2,1)S(1)} %collective-permute-done.3.refs_4_), channel_id=1, source_target_pairs={{0,16},{1,49},{2,18},{3,51},{4,20},{5,53},{6,22},{7,55},{8,24},{9,... | collective-permute-start | bytes 2433032 | tf_op jit(solution)/shard_map/ppermute | solution.py:59
  35.9 0.0 collective-permute-done.5.refs_6_
  35.9 1.5 collective-permute-start.7
  37.3 0.0 collective-permute-done.13.refs_14_
  37.3 0.0 collective-permute-start.8
  37.3 0.0 collective-permute-done.14.refs_15_
  37.3 0.0 copy-start.9
  37.4 0.1 collective-permute-start.10
  37.4 0.0 collective-permute-done.15.refs_16_
  37.5 0.1 collective-permute-start.11
  37.5 7.5 %collective-permute-done.6.refs_7_ = bf16[528,768]{1,0:T(8,128)(2,1)} collective-permute-done((bf16[528,768]{1,0:T(8,128)(2,1)S(1)}, bf16[528,768]{1,0:T(8,128)(2,1)}, u32[]{:S(2)}, u32[]{:S(2)}) %collective-permute-start.6) | collective-permute-done | bytes 811040 | tf_op jit(solution)/shard_map/ppermute | solution.py:59
  45.1 10.5 %collective-permute-start.16 = (bf16[528,768]{1,0:T(8,128)(2,1)S(1)}, bf16[528,768]{1,0:T(8,128)(2,1)S(1)}, u32[]{:S(2)}, u32[]{:S(2)}) collective-permute-start(bf16[528,768]{1,0:T(8,128)(2,1)S(1)} %collective-permute-done.3.refs_4_), channel_id=1, source_target_pairs={{0,1},{1,0},{2,3},{3,2},{4,5},{5,4},{6,7},{7,6},{8,9},{9,8},{10,11... | collective-permute-start | bytes 2433032 | tf_op jit(solution)/shard_map/ppermute | solution.py:63
  55.5 0.0 collective-permute-done.7.refs_8_
  55.5 3.9 %collective-permute-start.17 = (bf16[528,768]{1,0:T(8,128)(2,1)S(1)}, bf16[528,768]{1,0:T(8,128)(2,1)S(1)}, u32[]{:S(2)}, u32[]{:S(2)}) collective-permute-start(bf16[528,768]{1,0:T(8,128)(2,1)S(1)} %collective-permute-done.4.refs_5_), channel_id=1, source_target_pairs={{0,1},{1,0},{2,3},{3,2},{4,5},{5,4},{6,7},{7,6},{8,9},{9,8},{10,11... | collective-permute-start | bytes 2433032 | tf_op jit(solution)/shard_map/ppermute | solution.py:63
  59.4 0.0 collective-permute-done.8.refs_9_
  59.4 0.0 collective-permute-start.18
  59.4 0.0 collective-permute-done.10.refs_11_
  59.5 0.0 copy-start.11
  59.5 1.4 collective-permute-start.9
  60.9 0.0 collective-permute-done.11.refs_12_
  60.9 0.0 collective-permute-start.19
  60.9 0.0 collective-permute-done.16.refs_17_
  60.9 0.6 collective-permute-start.20
  61.5 1.0 collective-permute-done.17.refs_18_
  62.5 0.4 collective-permute-start.21
  62.8 0.0 copy-done.9
  62.9 0.0 copy-done.11
  62.9 0.5 copy-done.14
  63.4 0.7 copy-done
  64.1 0.0 copy-done.1
  64.1 0.1 pad_add_fusion
  64.2 0.5 add_add_fusion.where_ref
  64.7 0.0 collective-permute-done.18.refs_19_
  64.7 6.5 %collective-permute-done.9.refs_10_ = bf16[528,768]{1,0:T(8,128)(2,1)} collective-permute-done((bf16[528,768]{1,0:T(8,128)(2,1)}, bf16[528,768]{1,0:T(8,128)(2,1)}, u32[]{:S(2)}, u32[]{:S(2)}) %collective-permute-start.9) | collective-permute-done | bytes 811040 | tf_op jit(solution)/shard_map/ppermute | solution.py:59
  71.2 0.0 collective-permute-done.19.refs_20_
  71.2 0.0 collective-permute-done.20.refs_21_
  71.3 0.0 collective-permute-done.21.refs_22_
  71.3 0.0 copy-done.2
  71.3 0.0 copy-done.3
  71.3 0.0 copy-done.4
  71.3 0.0 copy-done.5
  71.3 91.2 %gram_13_23.1.found_ref = f32[23,512]{1,0:T(8,128)} custom-call(bf16[528,768]{1,0:T(8,128)(2,1)} %get-tuple-element.7.refs_0_, bf16[528,768]{1,0:T(8,128)(2,1)} %copy-done.4, bf16[528,768]{1,0:T(8,128)(2,1)} %copy-done.2, bf16[528,768]{1,0:T(8,128)(2,1)} %copy-done.3, bf16[528,768]{1,0:T(8,128)(2,1)} %copy-done.6, bf16[528,768]{1,0:T(8,128)(2,1)} %copy-done.7, ...), custom_call_target="tpu_custom_call" | custom-call | flops 18003148800 | bytes 18653184 | tf_op jit(solution)/shard_map/gram_13_23/pallas_call | solution.py:245
  162.5 1.6 scatter.1
  164.0 1.2 copy.4
  165.2 20.0 %all_to_all.11 = f32[128,1,512]{2,1,0:T(1,128)S(1)} all-to-all(f32[128,1,512]{2,1,0:T(1,128)S(1)} %copy.4), channel_id=1, replica_groups=mesh['group'=8,'row'=16] {'group','row'}, dimensions={0} | all-to-all | bytes 524288 | tf_op jit(solution)/shard_map/all_to_all | solution.py:321
  185.2 0.7 copy.7
  185.9 1.9 finish.1
  (22 shorter events, 0.0 us)
Async XLA Ops:
  3.2 14.7 %collective-permute-start.1 = (bf16[528,768]{1,0:T(8,128)(2,1)}, bf16[528,768]{1,0:T(8,128)(2,1)S(1)}, u32[]{:S(2)}, u32[]{:S(2)}) collective-permute-start(bf16[528,768]{1,0:T(8,128)(2,1)} %get-tuple-element.7.refs_0_), channel_id=1, source_target_pairs={{0,66},{1,5},{2,0},{3,7},{4,70},{5,9},{6,4},{7,11},{8,74},{9,13},{... | collective-permute-start | bytes 2433032 | tf_op jit(solution)/shard_map/ppermute | solution.py:59
  5.7 15.0 %collective-permute-start.2 = (bf16[528,768]{1,0:T(8,128)(2,1)}, bf16[528,768]{1,0:T(8,128)(2,1)S(1)}, u32[]{:S(2)}, u32[]{:S(2)}) collective-permute-start(bf16[528,768]{1,0:T(8,128)(2,1)} %get-tuple-element.7.refs_0_), channel_id=1, source_target_pairs={{0,16},{1,3},{2,18},{3,65},{4,20},{5,7},{6,22},{7,69},{8,24},{9,11... | collective-permute-start | bytes 2433032 | tf_op jit(solution)/shard_map/ppermute | solution.py:59
  7.0 16.2 %collective-permute-start = (bf16[528,768]{1,0:T(8,128)(2,1)}, bf16[528,768]{1,0:T(8,128)(2,1)S(1)}, u32[]{:S(2)}, u32[]{:S(2)}) collective-permute-start(bf16[528,768]{1,0:T(8,128)(2,1)} %get-tuple-element.7.refs_0_), channel_id=1, source_target_pairs={{0,48},{1,13},{2,50},{3,15},{4,52},{5,1},{6,54},{7,3},{8,56},{9,5}... | collective-permute-start | bytes 2433032 | tf_op jit(solution)/shard_map/ppermute | solution.py:59
  9.1 16.4 %collective-permute-start.12 = (bf16[528,768]{1,0:T(8,128)(2,1)}, bf16[528,768]{1,0:T(8,128)(2,1)S(1)}, u32[]{:S(2)}, u32[]{:S(2)}) collective-permute-start(bf16[528,768]{1,0:T(8,128)(2,1)} %get-tuple-element.7.refs_0_), channel_id=1, source_target_pairs={{0,1},{1,0},{2,3},{3,2},{4,5},{5,4},{6,7},{7,6},{8,9},{9,8},{10,11... | collective-permute-start | bytes 2433032 | tf_op jit(solution)/shard_map/ppermute | solution.py:63
  17.9 53.3 %copy-start.2 = (bf16[528,768]{1,0:T(8,128)(2,1)}, bf16[528,768]{1,0:T(8,128)(2,1)S(1)}, u32[]{:S(2)}) copy-start(bf16[528,768]{1,0:T(8,128)(2,1)S(1)} %collective-permute-done.1.refs_2_) | copy-start | bytes 2433028
  17.9 11.9 %collective-permute-start.3 = (bf16[528,768]{1,0:T(8,128)(2,1)S(1)}, bf16[528,768]{1,0:T(8,128)(2,1)S(1)}, u32[]{:S(2)}, u32[]{:S(2)}) collective-permute-start(bf16[528,768]{1,0:T(8,128)(2,1)S(1)} %collective-permute-done.1.refs_2_), channel_id=1, source_target_pairs={{0,4},{1,67},{2,6},{3,1},{4,8},{5,71},{6,10},{7,5},{8,12},{9,75},{... | collective-permute-start | bytes 2433032 | tf_op jit(solution)/shard_map/ppermute | solution.py:59
  20.7 50.6 %copy-start.3 = (bf16[528,768]{1,0:T(8,128)(2,1)}, bf16[528,768]{1,0:T(8,128)(2,1)S(1)}, u32[]{:S(2)}) copy-start(bf16[528,768]{1,0:T(8,128)(2,1)S(1)} %collective-permute-done.2.refs_3_) | copy-start | bytes 2433028
  20.7 11.7 %collective-permute-start.4 = (bf16[528,768]{1,0:T(8,128)(2,1)S(1)}, bf16[528,768]{1,0:T(8,128)(2,1)S(1)}, u32[]{:S(2)}, u32[]{:S(2)}) collective-permute-start(bf16[528,768]{1,0:T(8,128)(2,1)S(1)} %collective-permute-done.2.refs_3_), channel_id=1, source_target_pairs={{0,12},{1,49},{2,14},{3,51},{4,0},{5,53},{6,2},{7,55},{8,4},{9,57}... | collective-permute-start | bytes 2433032 | tf_op jit(solution)/shard_map/ppermute | solution.py:59
  23.1 48.1 %copy-start.4 = (bf16[528,768]{1,0:T(8,128)(2,1)}, bf16[528,768]{1,0:T(8,128)(2,1)S(1)}, u32[]{:S(2)}) copy-start(bf16[528,768]{1,0:T(8,128)(2,1)S(1)} %collective-permute-done.refs_1_) | copy-start | bytes 2433028
  23.1 12.7 %collective-permute-start.5 = (bf16[528,768]{1,0:T(8,128)(2,1)S(1)}, bf16[528,768]{1,0:T(8,128)(2,1)}, u32[]{:S(2)}, u32[]{:S(2)}) collective-permute-start(bf16[528,768]{1,0:T(8,128)(2,1)S(1)} %collective-permute-done.refs_1_), channel_id=1, source_target_pairs={{0,2},{1,17},{2,64},{3,19},{4,6},{5,21},{6,68},{7,23},{8,10},{9,25... | collective-permute-start | bytes 2433032 | tf_op jit(solution)/shard_map/ppermute | solution.py:59
  23.2 14.2 %collective-permute-start.13 = (bf16[528,768]{1,0:T(8,128)(2,1)S(1)}, bf16[528,768]{1,0:T(8,128)(2,1)S(1)}, u32[]{:S(2)}, u32[]{:S(2)}) collective-permute-start(bf16[528,768]{1,0:T(8,128)(2,1)S(1)} %collective-permute-done.refs_1_), channel_id=1, source_target_pairs={{0,1},{1,0},{2,3},{3,2},{4,5},{5,4},{6,7},{7,6},{8,9},{9,8},{10,11... | collective-permute-start | bytes 2433032 | tf_op jit(solution)/shard_map/ppermute | solution.py:63
  25.5 45.8 %copy-start.5 = (bf16[528,768]{1,0:T(8,128)(2,1)}, bf16[528,768]{1,0:T(8,128)(2,1)S(1)}, u32[]{:S(2)}) copy-start(bf16[528,768]{1,0:T(8,128)(2,1)S(1)} %collective-permute-done.12.refs_13_) | copy-start | bytes 2433028
  25.5 11.8 %collective-permute-start.14 = (bf16[528,768]{1,0:T(8,128)(2,1)S(1)}, bf16[528,768]{1,0:T(8,128)(2,1)S(1)}, u32[]{:S(2)}, u32[]{:S(2)}) collective-permute-start(bf16[528,768]{1,0:T(8,128)(2,1)S(1)} %collective-permute-done.1.refs_2_), channel_id=1, source_target_pairs={{0,1},{1,0},{2,3},{3,2},{4,5},{5,4},{6,7},{7,6},{8,9},{9,8},{10,11... | collective-permute-start | bytes 2433032 | tf_op jit(solution)/shard_map/ppermute | solution.py:63
  29.9 15.2 %copy-start.6 = (bf16[528,768]{1,0:T(8,128)(2,1)}, bf16[528,768]{1,0:T(8,128)(2,1)S(1)}, u32[]{:S(2)}) copy-start(bf16[528,768]{1,0:T(8,128)(2,1)S(1)} %collective-permute-done.3.refs_4_) | copy-start | bytes 2433028
  29.9 7.6 %collective-permute-start.15 = (bf16[528,768]{1,0:T(8,128)(2,1)S(1)}, bf16[528,768]{1,0:T(8,128)(2,1)S(1)}, u32[]{:S(2)}, u32[]{:S(2)}) collective-permute-start(bf16[528,768]{1,0:T(8,128)(2,1)S(1)} %collective-permute-done.2.refs_3_), channel_id=1, source_target_pairs={{0,1},{1,0},{2,3},{3,2},{4,5},{5,4},{6,7},{7,6},{8,9},{9,8},{10,11... | collective-permute-start | bytes 2433032 | tf_op jit(solution)/shard_map/ppermute | solution.py:63
  32.3 28.6 %copy-start.7 = (bf16[528,768]{1,0:T(8,128)(2,1)}, bf16[528,768]{1,0:T(8,128)(2,1)S(1)}, u32[]{:S(2)}) copy-start(bf16[528,768]{1,0:T(8,128)(2,1)S(1)} %collective-permute-done.4.refs_5_) | copy-start | bytes 2433028
  32.3 12.7 %collective-permute-start.6 = (bf16[528,768]{1,0:T(8,128)(2,1)S(1)}, bf16[528,768]{1,0:T(8,128)(2,1)}, u32[]{:S(2)}, u32[]{:S(2)}) collective-permute-start(bf16[528,768]{1,0:T(8,128)(2,1)S(1)} %collective-permute-done.3.refs_4_), channel_id=1, source_target_pairs={{0,16},{1,49},{2,18},{3,51},{4,20},{5,53},{6,22},{7,55},{8,24},{9,... | collective-permute-start | bytes 2433032 | tf_op jit(solution)/shard_map/ppermute | solution.py:59
  35.9 19.7 %collective-permute-start.7 = (bf16[528,768]{1,0:T(8,128)(2,1)S(1)}, bf16[528,768]{1,0:T(8,128)(2,1)}, u32[]{:S(2)}, u32[]{:S(2)}) collective-permute-start(bf16[528,768]{1,0:T(8,128)(2,1)S(1)} %collective-permute-done.4.refs_5_), channel_id=1, source_target_pairs={{0,2},{1,13},{2,64},{3,15},{4,6},{5,1},{6,68},{7,3},{8,10},{9,5},{... | collective-permute-start | bytes 2433032 | tf_op jit(solution)/shard_map/ppermute | solution.py:59
  37.3 25.1 %copy-start.8 = (bf16[528,768]{1,0:T(8,128)(2,1)}, bf16[528,768]{1,0:T(8,128)(2,1)S(1)}, u32[]{:S(2)}) copy-start(bf16[528,768]{1,0:T(8,128)(2,1)S(1)} %collective-permute-done.13.refs_14_) | copy-start | bytes 2433028
  37.3 22.1 %collective-permute-start.8 = (bf16[528,768]{1,0:T(8,128)(2,1)S(1)}, bf16[528,768]{1,0:T(8,128)(2,1)}, u32[]{:S(2)}, u32[]{:S(2)}) collective-permute-start(bf16[528,768]{1,0:T(8,128)(2,1)S(1)} %collective-permute-done.4.refs_5_), channel_id=1, source_target_pairs={{0,66},{1,5},{2,0},{3,7},{4,70},{5,9},{6,4},{7,11},{8,74},{9,13},{... | collective-permute-start | bytes 2433032 | tf_op jit(solution)/shard_map/ppermute | solution.py:59
  37.3 25.5 %copy-start.9 = (bf16[528,768]{1,0:T(8,128)(2,1)}, bf16[528,768]{1,0:T(8,128)(2,1)S(1)}, u32[]{:S(2)}) copy-start(bf16[528,768]{1,0:T(8,128)(2,1)S(1)} %collective-permute-done.14.refs_15_) | copy-start | bytes 2433028
  37.4 22.1 %collective-permute-start.10 = (bf16[528,768]{1,0:T(8,128)(2,1)}, bf16[528,768]{1,0:T(8,128)(2,1)S(1)}, u32[]{:S(2)}, u32[]{:S(2)}) collective-permute-start(bf16[528,768]{1,0:T(8,128)(2,1)} %collective-permute-done.5.refs_6_), channel_id=1, source_target_pairs={{0,4},{1,3},{2,6},{3,65},{4,8},{5,7},{6,10},{7,69},{8,12},{9,11},{... | collective-permute-start | bytes 2433032 | tf_op jit(solution)/shard_map/ppermute | solution.py:59
  37.5 25.4 %copy-start.10 = (bf16[528,768]{1,0:T(8,128)(2,1)}, bf16[528,768]{1,0:T(8,128)(2,1)S(1)}, u32[]{:S(2)}) copy-start(bf16[528,768]{1,0:T(8,128)(2,1)S(1)} %collective-permute-done.15.refs_16_) | copy-start | bytes 2433028
  37.5 23.4 %collective-permute-start.11 = (bf16[528,768]{1,0:T(8,128)(2,1)S(1)}, bf16[528,768]{1,0:T(8,128)(2,1)S(1)}, u32[]{:S(2)}, u32[]{:S(2)}) collective-permute-start(bf16[528,768]{1,0:T(8,128)(2,1)S(1)} %collective-permute-done.3.refs_4_), channel_id=1, source_target_pairs={{0,66},{1,17},{2,0},{3,19},{4,70},{5,21},{6,4},{7,23},{8,74},{9,25... | collective-permute-start | bytes 2433032 | tf_op jit(solution)/shard_map/ppermute | solution.py:59
  45.1 15.8 %collective-permute-start.16 = (bf16[528,768]{1,0:T(8,128)(2,1)S(1)}, bf16[528,768]{1,0:T(8,128)(2,1)S(1)}, u32[]{:S(2)}, u32[]{:S(2)}) collective-permute-start(bf16[528,768]{1,0:T(8,128)(2,1)S(1)} %collective-permute-done.3.refs_4_), channel_id=1, source_target_pairs={{0,1},{1,0},{2,3},{3,2},{4,5},{5,4},{6,7},{7,6},{8,9},{9,8},{10,11... | collective-permute-start | bytes 2433032 | tf_op jit(solution)/shard_map/ppermute | solution.py:63
  55.5 6.9 %collective-permute-start.17 = (bf16[528,768]{1,0:T(8,128)(2,1)S(1)}, bf16[528,768]{1,0:T(8,128)(2,1)S(1)}, u32[]{:S(2)}, u32[]{:S(2)}) collective-permute-start(bf16[528,768]{1,0:T(8,128)(2,1)S(1)} %collective-permute-done.4.refs_5_), channel_id=1, source_target_pairs={{0,1},{1,0},{2,3},{3,2},{4,5},{5,4},{6,7},{7,6},{8,9},{9,8},{10,11... | collective-permute-start | bytes 2433032 | tf_op jit(solution)/shard_map/ppermute | solution.py:63
  59.4 5.3 %collective-permute-start.18 = (bf16[528,768]{1,0:T(8,128)(2,1)}, bf16[528,768]{1,0:T(8,128)(2,1)}, u32[]{:S(2)}, u32[]{:S(2)}) collective-permute-start(bf16[528,768]{1,0:T(8,128)(2,1)} %collective-permute-done.5.refs_6_), channel_id=1, source_target_pairs={{0,1},{1,0},{2,3},{3,2},{4,5},{5,4},{6,7},{7,6},{8,9},{9,8},{10,11... | collective-permute-start | bytes 2433032 | tf_op jit(solution)/shard_map/ppermute | solution.py:63
  59.5 3.4 %copy-start.11 = (bf16[528,768]{1,0:T(8,128)(2,1)}, bf16[528,768]{1,0:T(8,128)(2,1)S(1)}, u32[]{:S(2)}) copy-start(bf16[528,768]{1,0:T(8,128)(2,1)S(1)} %collective-permute-done.10.refs_11_) | copy-start | bytes 2433028
  59.5 11.8 %collective-permute-start.9 = (bf16[528,768]{1,0:T(8,128)(2,1)}, bf16[528,768]{1,0:T(8,128)(2,1)}, u32[]{:S(2)}, u32[]{:S(2)}) collective-permute-start(bf16[528,768]{1,0:T(8,128)(2,1)} %collective-permute-done.5.refs_6_), channel_id=1, source_target_pairs={{0,48},{1,13},{2,50},{3,15},{4,52},{5,1},{6,54},{7,3},{8,56},{9,5}... | collective-permute-start | bytes 2433032 | tf_op jit(solution)/shard_map/ppermute | solution.py:59
  60.9 2.0 %copy-start.12 = (bf16[528,768]{1,0:T(8,128)(2,1)}, bf16[528,768]{1,0:T(8,128)(2,1)S(1)}, u32[]{:S(2)}) copy-start(bf16[528,768]{1,0:T(8,128)(2,1)S(1)} %collective-permute-done.11.refs_12_) | copy-start | bytes 2433028
  60.9 10.4 %collective-permute-start.19 = (bf16[528,768]{1,0:T(8,128)(2,1)}, bf16[528,768]{1,0:T(8,128)(2,1)}, u32[]{:S(2)}, u32[]{:S(2)}) collective-permute-start(bf16[528,768]{1,0:T(8,128)(2,1)} %collective-permute-done.6.refs_7_), channel_id=1, source_target_pairs={{0,1},{1,0},{2,3},{3,2},{4,5},{5,4},{6,7},{7,6},{8,9},{9,8},{10,11... | collective-permute-start | bytes 2433032 | tf_op jit(solution)/shard_map/ppermute | solution.py:63
  60.9 2.0 %copy-start.13 = (bf16[528,768]{1,0:T(8,128)(2,1)}, bf16[528,768]{1,0:T(8,128)(2,1)S(1)}, u32[]{:S(2)}) copy-start(bf16[528,768]{1,0:T(8,128)(2,1)S(1)} %collective-permute-done.16.refs_17_) | copy-start | bytes 2433028
  60.9 10.3 %collective-permute-start.20 = (bf16[528,768]{1,0:T(8,128)(2,1)}, bf16[528,768]{1,0:T(8,128)(2,1)}, u32[]{:S(2)}, u32[]{:S(2)}) collective-permute-start(bf16[528,768]{1,0:T(8,128)(2,1)} %collective-permute-done.7.refs_8_), channel_id=1, source_target_pairs={{0,1},{1,0},{2,3},{3,2},{4,5},{5,4},{6,7},{7,6},{8,9},{9,8},{10,11... | collective-permute-start | bytes 2433032 | tf_op jit(solution)/shard_map/ppermute | solution.py:63
  62.5 0.9 copy-start.14
  62.5 8.8 %collective-permute-start.21 = (bf16[528,768]{1,0:T(8,128)(2,1)}, bf16[528,768]{1,0:T(8,128)(2,1)}, u32[]{:S(2)}, u32[]{:S(2)}) collective-permute-start(bf16[528,768]{1,0:T(8,128)(2,1)} %collective-permute-done.8.refs_9_), channel_id=1, source_target_pairs={{0,1},{1,0},{2,3},{3,2},{4,5},{5,4},{6,7},{7,6},{8,9},{9,8},{10,11... | collective-permute-start | bytes 2433032 | tf_op jit(solution)/shard_map/ppermute | solution.py:63
  63.4 0.7 copy-start
  63.4 0.7 copy-start.1

commit v2 on v1

v2 whole, which is shorter than its diff:
```python
import functools

import jax
import jax.numpy as jnp
import numpy as np
from jax import lax
from jax.experimental import pallas as pl
from jax.experimental.pallas import tpu as pltpu
from jax.sharding import PartitionSpec as P

D = 768
RB = 512
GROUPS = 8
META = 16
SENT = RB + META
HELD = 640
SHORT, LONG = 80, 144
TILE = 256
STRIP = 512
ABSENT = -4.0
LOW = -1e30
AXES = ("group", "row")

UNIT = ((1, 0, 0), (0, 1, 0), (0, 0, 1), (3, 0, 0), (0, 3, 0), (0, 0, 3))
PARENT = (None,) + (0, 0, 0, 1, 2, 0, 5, 4, 1, 8, 9, 6)
DIRS = (
    (None,) + (5, 3, 2, 1, 4, 0, 4, 3, 5, 5, 0, 2),
    (None,) + (1, 0, 4, 5, 2, 3, 2, 0, 1, 1, 3, 4),
)
SLOTS = len(PARENT)
OTHER = 20
MEETINGS = (
    ((0, 3, 23), (1, 2), True),
    ((4, 5, 6), (0, 2, 3, 20, 21, 22, 23, 25, 26), True),
    ((7, 8, 9), (0, 1, 2, 3, 4, 5, 6, 22, 24, 25, 26, 27, 29), True),
    ((10, 11, 12), (2, 5, 7, 23, 24, 26, 29), False),
)
NAMES = tuple(sorted({k for meeting in MEETINGS for k in meeting[0] + meeting[1]}))


def offsets():
    table = []
    for core in range(2):
        held = [(0, 0, 0)]
        for i in range(1, SLOTS):
            step, base = UNIT[DIRS[core][i]], held[PARENT[i]]
            held.append(tuple((a + b) % 4 for a, b in zip(step, base)))
        table.append(held)
    return table


def place(x, y, z, core):
    group = (y // 2) * 4 + x
    row = (z * 2 + y % 2) * 2 + core
    return group * 16 + row


def fetch(block, steps):
    pairs = []
    for x in range(4):
        for y in range(4):
            for z in range(4):
                for core in range(2):
                    dx, dy, dz = steps[core]
                    source = place((x + dx) % 4, (y + dy) % 4, (z + dz) % 4, core)
                    pairs.append((source, place(x, y, z, core)))
    return lax.ppermute(block, AXES, sorted(pairs))


def flip(block):
    return lax.ppermute(block, AXES, [(i, i ^ 1) for i in range(128)])


def prepare_kernel(embeds_ref, member_ref, block_ref, target_ref):
    member = member_ref[...].astype(jnp.float32)
    column = jnp.transpose(jnp.broadcast_to(member, (128, RB)))[:, 0:1]
    above = lax.broadcasted_iota(jnp.int32, (RB, RB), 0)
    across = lax.broadcasted_iota(jnp.int32, (RB, RB), 1)
    before = (column < member) | ((column == member) & (above < across))
    target = jnp.sum(before.astype(jnp.float32), axis=0, keepdims=True).astype(jnp.int32)
    target_ref[...] = target
    values = embeds_ref[...].astype(jnp.float32)
    total = jnp.sum(values * values, axis=1, keepdims=True)
    normed = (values * lax.rsqrt(total + 1e-06)).astype(jnp.bfloat16)
    placer = (above == target).astype(jnp.bfloat16)
    block_ref[0:RB, :] = jnp.dot(placer, normed, preferred_element_type=jnp.float32).astype(
        jnp.bfloat16
    )
    lane = lax.broadcasted_iota(jnp.int32, (RB, D), 1).astype(jnp.float32)
    counts = jnp.sum((column == lane).astype(jnp.float32), axis=0, keepdims=True)
    block_ref[RB:SENT, :] = jnp.broadcast_to(counts, (META, D)).astype(jnp.bfloat16)


def prepare(embeds, member):
    return pl.pallas_call(
        prepare_kernel,
        out_shape=(
            jax.ShapeDtypeStruct((SENT, D), jnp.bfloat16),
            jax.ShapeDtypeStruct((1, RB), jnp.int32),
        ),
        name="prepare",
    )(embeds, member.reshape(1, RB))


def gram_kernel(new, total, among, lists, *refs):
    blocks, refs = refs[:total], refs[total:]
    if lists:
        where_ref, refs = refs[0], refs[1:]
        before, refs = refs[: len(lists) - 1], refs[len(lists) - 1 :]
    out_ref, refs = refs[0], refs[1:]
    (held, rows, bias, best, kept, turned, counts_v, counts_s, start_s, put_s, sems, meta_sem) = (
        refs
    )
    copies = []
    for k in range(total):
        copy = pltpu.make_async_copy(blocks[k], held.at[k, pl.ds(0, SENT)], sems.at[k])
        copy.start()
        copies.append(copy)
    rows[...] = jnp.zeros_like(rows)
    for k in range(total):
        held[k, SENT:HELD, :] = jnp.zeros((HELD - SENT, D), jnp.bfloat16)
        kept[k] = jnp.full((HELD, 128), LOW, jnp.float32)
        start_s[k] = 0
    for k in range(total):
        copies[k].wait()
        counts_v[k : k + 1, :] = held[k, RB:SENT, 0:128].astype(jnp.float32)[0:1].astype(jnp.int32)
    fetch_counts = pltpu.make_async_copy(counts_v, counts_s, meta_sem)
    fetch_counts.start()
    fetch_counts.wait()

    def segment(k, c):
        low = start_s[k]
        high = low + counts_s[k, c]
        first = pl.multiple_of((low // 16) * 16, 16)
        tiles = jnp.where(high > low, (high - first + 15) // 16, 0)
        return low, high, first, tiles

    def bias_of(length, first, low, high):
        at = first + lax.broadcasted_iota(jnp.int32, (length, 128), 0)
        return jnp.where((at >= low) & (at < high), 0.0, LOW)

    def one_cluster(c, carry):
        put = jnp.int32(0)
        new_rows = put
        for k in range(total):
            low, high, first, tiles = segment(k, c)
            put = pl.multiple_of(put, 16)
            put_s[k] = put

            def gather(skip, length, k=k, low=low, high=high, first=first, put=put):
                source = pl.multiple_of(first + skip, 16)
                at = pl.multiple_of(put + skip, 16)
                rows[pl.ds(at, length), :] = held[k, pl.ds(source, length), :]
                bias[pl.ds(at, length), :] = bias_of(length, source, low, high)

            pl.when(tiles > 0)(functools.partial(gather, 0, SHORT))
            pl.when(tiles > SHORT // 16)(functools.partial(gather, SHORT, LONG - SHORT))
            put = put + tiles * 16
            if k == new - 1:
                new_rows = put
        put = pl.multiple_of(put, 16)
        bias[pl.ds(put, STRIP), :] = jnp.full((STRIP, 128), LOW, jnp.float32)

        def clear(m, carry):
            at = pl.multiple_of(m * TILE, TILE)
            best[pl.ds(at, TILE), :] = jnp.full((TILE, 128), LOW, jnp.float32)
            return carry

        lax.fori_loop(0, (put + STRIP + TILE - 1) // TILE, clear, 0)

        def one_column_tile(n, carry):
            here = pl.multiple_of(n * TILE, TILE)
            turned[...] = jnp.transpose(rows[pl.ds(here, TILE), :])
            inside = here + lax.broadcasted_iota(jnp.int32, (1, TILE), 1) < new_rows
            column_bias = jnp.transpose(bias[pl.ds(here, TILE), :])[0:1, :]
            column_bias = jnp.where(inside, column_bias, LOW)

            def visit(at, length, diagonal, column_best):
                scores = jnp.dot(
                    rows[pl.ds(at, length), :], turned[...], preferred_element_type=jnp.float32
                )
                if diagonal:
                    same = lax.broadcasted_iota(jnp.int32, (TILE, TILE), 0)
                    same = same == lax.broadcasted_iota(jnp.int32, (TILE, TILE), 1)
                    scores = jnp.where(same, LOW, scores)
                masked = scores + column_bias
                best[pl.ds(at, length), :] = jnp.maximum(
                    best[pl.ds(at, length), :],
                    jnp.maximum(masked[:, :128], masked[:, 128:]),
                )
                row_bias = bias[pl.ds(at, length), :]
                masked = scores + jnp.concatenate([row_bias, row_bias], axis=1)
                top = jnp.max(masked.reshape(length // 8, 8, TILE), axis=0)
                return jnp.maximum(column_best, top)

            column_best = jnp.full((8, TILE), LOW, jnp.float32)
            if among:
                column_best = visit(here, TILE, True, column_best)
                rest = pl.multiple_of(here + TILE, 16)
            else:
                rest = pl.multiple_of(new_rows, 16)

            def strip(i, column_best):
                at = pl.multiple_of(rest + i * STRIP, 16)
                return visit(at, STRIP, False, column_best)

            strips = jnp.maximum(put - rest + STRIP - 1, 0) // STRIP
            column_best = lax.fori_loop(0, strips, strip, column_best)
            top = jnp.where(inside, jnp.max(column_best, axis=0, keepdims=True), LOW)
            down = jnp.transpose(jnp.broadcast_to(top, (128, TILE)))
            best[pl.ds(here, TILE), :] = jnp.maximum(best[pl.ds(here, TILE), :], down)
            return carry

        lax.fori_loop(0, (new_rows + TILE - 1) // TILE, one_column_tile, 0)

        for k in range(total):
            low, high, first, tiles = segment(k, c)
            put = pl.multiple_of(put_s[k], 16)

            def keep(skip, length, k=k, low=low, high=high, first=first, put=put):
                at = pl.multiple_of(first + skip, 16)
                source = pl.multiple_of(put + skip, 16)
                fresh = best[pl.ds(source, length), :] + bias_of(length, at, low, high)
                kept[k, pl.ds(at, length), :] = jnp.maximum(kept[k, pl.ds(at, length), :], fresh)

            pl.when(tiles > 0)(functools.partial(keep, 0, SHORT))
            pl.when(tiles > SHORT // 16)(functools.partial(keep, SHORT, LONG - SHORT))
            start_s[k] = high
        return carry

    lax.fori_loop(0, GROUPS, one_cluster, 0)

    def found_in(k):
        return jnp.max(jnp.transpose(kept[k, 0:RB, :]), axis=0, keepdims=True)

    if not lists:
        for k in range(total):
            out_ref[k : k + 1, :] = found_in(k)
        return
    out_ref[...] = jnp.full_like(out_ref, ABSENT)
    for number, name in enumerate(NAMES):
        found = jnp.full((1, RB), ABSENT, jnp.float32)
        if name in lists[0]:
            found = jnp.maximum(found, found_in(lists[0].index(name)))
        for ref, names in zip(before, lists[1:]):
            if name in names:
                at = names.index(name)
                found = jnp.maximum(found, ref[at : at + 1, :])
        out_ref[where_ref[number]] = found


def gram(blocks, new, among, lists=(), where=None, before=()):
    total = len(blocks)
    deep = -(-(total * LONG) // TILE) * TILE + 2 * STRIP
    shape = (128, 1, RB) if lists else (total, RB)
    in_specs = [pl.BlockSpec(memory_space=pl.ANY)] * total
    if lists:
        in_specs += [pl.BlockSpec(memory_space=pltpu.SMEM)]
        in_specs += [pl.BlockSpec(memory_space=pltpu.VMEM)] * len(before)
    return pl.pallas_call(
        functools.partial(gram_kernel, new, total, among, lists),
        out_shape=jax.ShapeDtypeStruct(shape, jnp.float32),
        in_specs=in_specs,
        scratch_shapes=[
            pltpu.VMEM((total, HELD, D), jnp.bfloat16),
            pltpu.VMEM((deep, D), jnp.bfloat16),
            pltpu.VMEM((deep, 128), jnp.float32),
            pltpu.VMEM((deep, 128), jnp.float32),
            pltpu.VMEM((total, HELD, 128), jnp.float32),
            pltpu.VMEM((D, TILE), jnp.bfloat16),
            pltpu.VMEM((total, 128), jnp.int32),
            pltpu.SMEM((total, 128), jnp.int32),
            pltpu.SMEM((total,), jnp.int32),
            pltpu.SMEM((total,), jnp.int32),
            pltpu.SemaphoreType.DMA((total,)),
            pltpu.SemaphoreType.DMA,
        ],
        compiler_params=pltpu.CompilerParams(vmem_limit_bytes=48 * 2**20),
        cost_estimate=pl.CostEstimate(
            flops=2 * GROUPS * 160 * 160 * D * new * total,
            bytes_accessed=total * SENT * D * 2,
            transcendentals=0,
        ),
        name=f"gram_{new}_{total}",
    )(*blocks, *(() if where is None else (where,)), *before)


def finish_kernel(arrived_ref, target_ref, out_ref):
    best = jnp.max(arrived_ref[...], axis=0, keepdims=True)
    column = jnp.transpose(jnp.broadcast_to(best, (128, RB)))[:, 0:1]
    above = lax.broadcasted_iota(jnp.int32, (RB, RB), 0)
    picked = jnp.where(above == target_ref[...], column, LOW)
    out_ref[...] = jnp.max(picked, axis=0, keepdims=True)


def finish(arrived, target):
    return pl.pallas_call(
        finish_kernel, out_shape=jax.ShapeDtypeStruct((1, RB), jnp.float32), name="finish"
    )(arrived, target)


def homes():
    group, row = lax.axis_index("group"), lax.axis_index("row")
    x, y, z, core = group % 4, (group // 4) * 2 + (row // 2) % 2, row // 4, row % 2
    table = jnp.array(offsets(), jnp.int32)
    own = jnp.where(core == 0, table[0], table[1])
    other = jnp.where(core == 0, table[1], table[0])
    names = np.array(NAMES)
    steps = jnp.where((names < OTHER)[:, None], own[names % OTHER], other[names % OTHER])
    cores = jnp.where(names < OTHER, core, 1 - core)
    at = place((x + steps[:, 0]) % 4, (y + steps[:, 1]) % 4, (z + steps[:, 2]) % 4, cores)
    return at.astype(jnp.int32)


def on_device(embeds, member):
    block, target = prepare(embeds, member)
    held = {0: block}
    for i in range(1, SLOTS):
        held[i] = fetch(held[PARENT[i]], (UNIT[DIRS[0][i]], UNIT[DIRS[1][i]]))
    for name in NAMES:
        if name >= OTHER:
            held[name] = flip(held[name - OTHER])
    before, lists = [], []
    for columns, beside, among in MEETINGS[:-1]:
        names = columns + beside
        before.append(gram([held[k] for k in names], len(columns), among))
        lists.append(names)
    columns, beside, among = MEETINGS[-1]
    lists = [columns + beside] + lists
    outgoing = gram(
        [held[k] for k in lists[0]], len(columns), among, tuple(lists), homes(), tuple(before)
    )
    arrived = lax.all_to_all(outgoing, AXES, split_axis=0, concat_axis=0, tiled=True)
    return finish(arrived.reshape(128, RB), target).reshape(-1)


def solution(mesh):
    in_specs = (P(AXES, None), P(AXES))
    return jax.shard_map(
        on_device, mesh=mesh, in_specs=in_specs, out_specs=P(AXES), check_vma=False
    )
```

time: 189 us -> 171 us (0.905)
  waiting for transfers between devices: 26.6 us -> 19.3 us
  starting transfers between devices: 39.5 us -> 34.1 us
  Pallas kernels: 97.8 us -> 93.4 us
  blocking collectives: 20 us -> 15.8 us
  local copies, waits for them, and re-layouts: 3.2 us -> 6.32 us
    ppermute x10 -> x9, starting transfers between devices: 21.9 us -> 8.91 us  [flip(): return lax.ppermute(block, AXES, [(i, i ^ 1) for i in range(128)])]
    ppermute x12, starting transfers between devices: 17.6 us -> 25.2 us  [fetch(): return lax.ppermute(block, AXES, sorted(pairs))]
    ppermute x12, waiting for transfers between devices: 25.5 us -> 19.3 us  [fetch(): return lax.ppermute(block, AXES, sorted(pairs))]
    pallas_call x2 -> x4, Pallas kernels: 92.7 us -> 88.3 us  [gram(): pl.pallas_call(functools.partial(gram_kernel, new, total, among, lists),...]
    all_to_all x1, blocking collectives: 20 us -> 15.8 us  [on_device(): lax.all_to_all(outgoing, AXES, split_axis=0, concat_axis=0, tiled=True)]
    unnamed x31 -> x23, local copies, waits for them, and re-layouts: 1.97 us -> 5 us
  transfers between devices with their start and end apart: 22 -> 21, of which waited for: 6 -> 3; matrix products, arithmetic and copies ran while one was open for 0% -> 1% of each run, Pallas kernels for 0% -> 39%
where the time goes in v2:
time: 171 us; the launch traced here: 169 us
  Pallas kernels  93.4 us (55%)
  starting transfers between devices  34.1 us (20%)
  waiting for transfers between devices  19.3 us (11%)
  blocking collectives  15.8 us (9%)
  local copies, waits for them, and re-layouts  6.32 us (4%)
    pallas_call x4, Pallas kernels, gram(): pl.pallas_call(functools.partial(gram_kernel, new, total, among, lists),...  88.3 us
    ppermute x12, starting transfers between devices, fetch(): return lax.ppermute(block, AXES, sorted(pairs))  25.2 us
    ppermute x12, waiting for transfers between devices, fetch(): return lax.ppermute(block, AXES, sorted(pairs))  19.3 us
    all_to_all x1, blocking collectives, on_device(): lax.all_to_all(outgoing, AXES, split_axis=0, concat_axis=0, tiled=True)  15.8 us
    ppermute x9, starting transfers between devices, flip(): return lax.ppermute(block, AXES, [(i, i ^ 1) for i in range(128)])  8.91 us
    unnamed x23, local copies, waits for them, and re-layouts  5 us
  transfers between devices with their start and end apart: 21, of which 3 were waited for; matrix products, arithmetic and copies ran while one was open for 1% of the time, Pallas kernels for 39%

profile of v2, /device:TPU:1, one launch (start us, length us, event | category | flops | bytes accessed | tf_op | source)
XLA Modules:
  0.0 169.5 jit_solution(14977221128161831985)
XLA Ops:
  0.0 3.2 %prepare.1 = (bf16[528,768]{1,0:T(8,128)(2,1)}, s32[1,512]{1,0:T(1,128)}) custom-call(bf16[512,768]{1,0:T(8,128)(2,1)} %embeds_ref.1, s32[1,512]{1,0:T(1,128)} %bitcast.10), custom_call_target="tpu_custom_call" | custom-call | tf_op jit(solution)/shard_map/prepare/pallas_call | solution.py:95
  3.2 3.3 %collective-permute-start.8 = (bf16[528,768]{1,0:T(8,128)(2,1)}, bf16[528,768]{1,0:T(8,128)(2,1)S(1)}, u32[]{:S(2)}, u32[]{:S(2)}) collective-permute-start(bf16[528,768]{1,0:T(8,128)(2,1)} %get-tuple-element.7.refs_0_.refs_3_), channel_id=1, source_target_pairs={{0,16},{1,49},{2,18},{3,51},{4,20},{5,53},{6,22},{7,55},{8,24},{9,... | collective-permute-start | bytes 2433032 | tf_op jit(solution)/shard_map/ppermute | solution.py:67
  6.5 2.7 %collective-permute-start = (bf16[528,768]{1,0:T(8,128)(2,1)}, bf16[528,768]{1,0:T(8,128)(2,1)S(1)}, u32[]{:S(2)}, u32[]{:S(2)}) collective-permute-start(bf16[528,768]{1,0:T(8,128)(2,1)} %get-tuple-element.7.refs_0_.refs_3_), channel_id=1, source_target_pairs={{0,4},{1,67},{2,6},{3,1},{4,8},{5,71},{6,10},{7,5},{8,12},{9,75},{... | collective-permute-start | bytes 2433032 | tf_op jit(solution)/shard_map/ppermute | solution.py:67
  9.3 0.0 collective-permute-start.6
  9.3 0.0 collective-permute-start.11
  9.3 2.7 %collective-permute-start.16 = (bf16[528,768]{1,0:T(8,128)(2,1)}, bf16[528,768]{1,0:T(8,128)(2,1)}, u32[]{:S(2)}, u32[]{:S(2)}) collective-permute-start(bf16[528,768]{1,0:T(8,128)(2,1)} %get-tuple-element.7.refs_0_.refs_3_), channel_id=1, source_target_pairs={{0,1},{1,0},{2,3},{3,2},{4,5},{5,4},{6,7},{7,6},{8,9},{9,8},{10,11... | collective-permute-start | bytes 2433032 | tf_op jit(solution)/shard_map/ppermute | solution.py:71
  12.0 9.1 %collective-permute-done.8.refs_4_.refs_5_.refs_3_ = bf16[528,768]{1,0:T(8,128)(2,1)S(1)} collective-permute-done((bf16[528,768]{1,0:T(8,128)(2,1)}, bf16[528,768]{1,0:T(8,128)(2,1)S(1)}, u32[]{:S(2)}, u32[]{:S(2)}) %collective-permute-start.8) | collective-permute-done | bytes 811040 | tf_op jit(solution)/shard_map/ppermute | solution.py:67
  21.1 5.7 %collective-permute-start.9 = (bf16[528,768]{1,0:T(8,128)(2,1)S(1)}, bf16[528,768]{1,0:T(8,128)(2,1)S(1)}, u32[]{:S(2)}, u32[]{:S(2)}) collective-permute-start(bf16[528,768]{1,0:T(8,128)(2,1)S(1)} %collective-permute-done.8.refs_4_.refs_5_.refs_3_), channel_id=1, source_target_pairs={{0,2},{1,13},{2,64},{3,15},{4,6},{5,1},{6,68},{7,3},{8,10},{9,5},{... | collective-permute-start | bytes 2433032 | tf_op jit(solution)/shard_map/ppermute | solution.py:67
  26.8 0.0 collective-permute-done.refs_3_.refs_4_
  26.8 0.0 collective-permute-start.1
  26.8 0.0 collective-permute-done.6.refs_2_.refs_9_
  26.8 2.8 %collective-permute-start.4 = (bf16[528,768]{1,0:T(8,128)(2,1)S(1)}, bf16[528,768]{1,0:T(8,128)(2,1)}, u32[]{:S(2)}, u32[]{:S(2)}) collective-permute-start(bf16[528,768]{1,0:T(8,128)(2,1)S(1)} %collective-permute-done.refs_3_.refs_4_), channel_id=1, source_target_pairs={{0,4},{1,67},{2,6},{3,1},{4,8},{5,71},{6,10},{7,5},{8,12},{9,75},{... | collective-permute-start | bytes 2433032 | tf_op jit(solution)/shard_map/ppermute | solution.py:67
  29.6 0.0 collective-permute-done.11.refs_1_.refs_5_.refs_6_
  29.6 0.5 collective-permute-start.12
  30.2 0.7 copy-done.6
  30.9 0.0 copy-done.5
  30.9 0.1 copy.16
  31.0 0.1 copy.17
  31.1 0.6 copy-done.7
  31.6 0.6 gather_fusion
  32.2 0.0 copy-start.4
  32.2 0.6 gather_fusion.1
  32.8 0.0 collective-permute-done.16.refs_6_
  32.8 0.1 collective-permute-start.18
  32.9 3.1 %collective-permute-done.9.refs_1_.refs_8_.refs_4_ = bf16[528,768]{1,0:T(8,128)(2,1)S(1)} collective-permute-done((bf16[528,768]{1,0:T(8,128)(2,1)S(1)}, bf16[528,768]{1,0:T(8,128)(2,1)S(1)}, u32[]{:S(2)}, u32[]{:S(2)}) %collective-permute-start.9) | collective-permute-done | bytes 811040 | tf_op jit(solution)/shard_map/ppermute | solution.py:67
  36.0 2.5 %collective-permute-start.17 = (bf16[528,768]{1,0:T(8,128)(2,1)S(1)}, bf16[528,768]{1,0:T(8,128)(2,1)}, u32[]{:S(2)}, u32[]{:S(2)}) collective-permute-start(bf16[528,768]{1,0:T(8,128)(2,1)S(1)} %collective-permute-done.refs_3_.refs_4_), channel_id=1, source_target_pairs={{0,1},{1,0},{2,3},{3,2},{4,5},{5,4},{6,7},{7,6},{8,9},{9,8},{10,11... | collective-permute-start | bytes 2433032 | tf_op jit(solution)/shard_map/ppermute | solution.py:71
  38.5 7.0 %collective-permute-done.1.refs_0_.refs_7_ = bf16[528,768]{1,0:T(8,128)(2,1)} collective-permute-done((bf16[528,768]{1,0:T(8,128)(2,1)S(1)}, bf16[528,768]{1,0:T(8,128)(2,1)}, u32[]{:S(2)}, u32[]{:S(2)}) %collective-permute-start.1) | collective-permute-done | bytes 811040 | tf_op jit(solution)/shard_map/ppermute | solution.py:67
  45.5 2.0 %collective-permute-start.14 = (bf16[528,768]{1,0:T(8,128)(2,1)S(1)}, bf16[528,768]{1,0:T(8,128)(2,1)}, u32[]{:S(2)}, u32[]{:S(2)}) collective-permute-start(bf16[528,768]{1,0:T(8,128)(2,1)S(1)} %collective-permute-done.6.refs_2_.refs_9_), channel_id=1, source_target_pairs={{0,1},{1,0},{2,3},{3,2},{4,5},{5,4},{6,7},{7,6},{8,9},{9,8},{10,11... | collective-permute-start | bytes 2433032 | tf_op jit(solution)/shard_map/ppermute | solution.py:71
  47.5 0.0 collective-permute-done.4.refs_2_
  47.5 3.3 %collective-permute-start.10 = (bf16[528,768]{1,0:T(8,128)(2,1)S(1)}, bf16[528,768]{1,0:T(8,128)(2,1)}, u32[]{:S(2)}, u32[]{:S(2)}) collective-permute-start(bf16[528,768]{1,0:T(8,128)(2,1)S(1)} %collective-permute-done.9.refs_1_.refs_8_.refs_4_), channel_id=1, source_target_pairs={{0,2},{1,13},{2,64},{3,15},{4,6},{5,1},{6,68},{7,3},{8,10},{9,5},{... | collective-permute-start | bytes 2433032 | tf_op jit(solution)/shard_map/ppermute | solution.py:67
  50.8 0.0 collective-permute-done.12.refs_2_.refs_9_.refs_6_
  50.8 0.0 collective-permute-start.19
  50.8 0.1 broadcast_select_fusion
  50.8 0.2 fusion.2
  51.1 0.0 copy-start
  51.1 1.1 copy-done
  52.2 14.3 %gram_3_5.1.refs_11_ = f32[5,512]{1,0:T(8,128)S(1)} custom-call(bf16[528,768]{1,0:T(8,128)(2,1)S(1)} %copy-done, bf16[528,768]{1,0:T(8,128)(2,1)} %collective-permute-done.11.refs_1_.refs_5_.refs_6_, bf16[528,768]{1,0:T(8,128)(2,1)} %collective-permute-done.12.refs_2_.refs_9_.refs_6_, bf16[528,768]{1,0:T(8,128)(2,1)S(1)} %collective-permute-done.refs_3_.refs_4_, ...), custom_call_target="tpu_custom_call" | custom-call | flops 4718592000 | bytes 4055040 | tf_op jit(solution)/shard_map/gram_3_5/pallas_call | solution.py:260
  66.6 0.0 collective-permute-done.18.refs_8_.refs_10_
  66.6 1.4 collective-permute-start.7
  67.9 0.0 collective-permute-done.14.refs_11_.refs_13_.refs_8_
  67.9 0.6 collective-permute-start.13
  68.5 0.0 collective-permute-done.17.refs_7_
  68.5 2.6 %collective-permute-start.2 = (bf16[528,768]{1,0:T(8,128)(2,1)}, bf16[528,768]{1,0:T(8,128)(2,1)S(1)}, u32[]{:S(2)}, u32[]{:S(2)}) collective-permute-start(bf16[528,768]{1,0:T(8,128)(2,1)} %collective-permute-done.1.refs_0_.refs_7_), channel_id=1, source_target_pairs={{0,16},{1,49},{2,18},{3,51},{4,20},{5,53},{6,22},{7,55},{8,24},{9,... | collective-permute-start | bytes 2433032 | tf_op jit(solution)/shard_map/ppermute | solution.py:67
  71.1 0.0 collective-permute-done.10.refs_0_.refs_5_
  71.1 0.0 collective-permute-start.15
  71.2 0.0 collective-permute-done.19.refs_10_.refs_12_
  71.2 0.5 collective-permute-start.20
  71.7 23.7 %gram_3_12.1.refs_12_ = f32[12,512]{1,0:T(8,128)S(1)} custom-call(bf16[528,768]{1,0:T(8,128)(2,1)} %collective-permute-done.1.refs_0_.refs_7_, bf16[528,768]{1,0:T(8,128)(2,1)S(1)} %collective-permute-done.9.refs_1_.refs_8_.refs_4_, bf16[528,768]{1,0:T(8,128)(2,1)S(1)} %collective-permute-done.6.refs_2_.refs_9_, bf16[528,768]{1,0:T(8,128)(2,1)S(1)} %copy-done, ...), custom_call_target="tpu_custom_call" | custom-call | flops 11324620800 | bytes 9732096 | tf_op jit(solution)/shard_map/gram_3_12/pallas_call | solution.py:260
  95.4 0.0 collective-permute-done.13.refs_11_.refs_7_
  95.4 0.1 collective-permute-start.5
  95.5 0.0 collective-permute-done.2.refs_1_
  95.5 3.4 %collective-permute-start.3 = (bf16[528,768]{1,0:T(8,128)(2,1)S(1)}, bf16[528,768]{1,0:T(8,128)(2,1)S(1)}, u32[]{:S(2)}, u32[]{:S(2)}) collective-permute-start(bf16[528,768]{1,0:T(8,128)(2,1)S(1)} %collective-permute-done.2.refs_1_), channel_id=1, source_target_pairs={{0,4},{1,67},{2,6},{3,1},{4,8},{5,71},{6,10},{7,5},{8,12},{9,75},{... | collective-permute-start | bytes 2433032 | tf_op jit(solution)/shard_map/ppermute | solution.py:67
  98.9 0.0 collective-permute-done.15.refs_15_.refs_9_
  98.9 0.0 collective-permute-done.20.refs_14_
  98.9 1.0 copy-done.9
  99.9 0.9 copy-done.10
  100.8 28.2 %gram_3_16.1.refs_13_ = f32[16,512]{1,0:T(8,128)S(1)} custom-call(bf16[528,768]{1,0:T(8,128)(2,1)} %collective-permute-done.10.refs_0_.refs_5_, bf16[528,768]{1,0:T(8,128)(2,1)S(1)} %collective-permute-done.2.refs_1_, bf16[528,768]{1,0:T(8,128)(2,1)} %collective-permute-done.4.refs_2_, bf16[528,768]{1,0:T(8,128)(2,1)S(1)} %copy-done, ...), custom_call_target="tpu_custom_call" | custom-call | flops 15099494400 | bytes 12976128 | tf_op jit(solution)/shard_map/gram_3_16/pallas_call | solution.py:260
  129.0 0.0 collective-permute-done.7.refs_2_
  129.0 0.0 collective-permute-done.5.refs_1_
  129.0 0.0 collective-permute-done.3.refs_0_
  129.0 22.0 %gram_3_10.1 = f32[128,1,512]{2,1,0:T(1,128)S(1)} custom-call(bf16[528,768]{1,0:T(8,128)(2,1)S(1)} %collective-permute-done.3.refs_0_, bf16[528,768]{1,0:T(8,128)(2,1)S(1)} %collective-permute-done.5.refs_1_, bf16[528,768]{1,0:T(8,128)(2,1)S(1)} %collective-permute-done.7.refs_2_, bf16[528,768]{1,0:T(8,128)(2,1)S(1)} %collective-permute-done.8.refs_4_.refs_5_.refs_3_, ...), custom_call_target="tpu_custom_call" | custom-call | flops 9437184000 | bytes 8110080 | tf_op jit(solution)/shard_map/gram_3_10/pallas_call | solution.py:260
  151.1 15.8 %all_to_all.5 = f32[128,1,512]{2,1,0:T(1,128)S(1)} all-to-all(f32[128,1,512]{2,1,0:T(1,128)S(1)} %gram_3_10.1), channel_id=1, replica_groups=mesh['group'=8,'row'=16] {'group','row'}, dimensions={0} | all-to-all | bytes 524288 | tf_op jit(solution)/shard_map/all_to_all | solution.py:333
  166.9 0.7 copy.20
  167.6 1.9 %finish.1 = f32[1,512]{1,0:T(1,128)} custom-call(f32[128,512]{1,0:T(8,128)} %bitcast.9, s32[1,512]{1,0:T(1,128)} %get-tuple-element.8.target_ref), custom_call_target="tpu_custom_call" | custom-call | tf_op jit(solution)/shard_map/finish/pallas_call | solution.py:297
  (17 shorter events, 0.1 us)
Async XLA Ops:
  3.2 17.9 %collective-permute-start.8 = (bf16[528,768]{1,0:T(8,128)(2,1)}, bf16[528,768]{1,0:T(8,128)(2,1)S(1)}, u32[]{:S(2)}, u32[]{:S(2)}) collective-permute-start(bf16[528,768]{1,0:T(8,128)(2,1)} %get-tuple-element.7.refs_0_.refs_3_), channel_id=1, source_target_pairs={{0,16},{1,49},{2,18},{3,51},{4,20},{5,53},{6,22},{7,55},{8,24},{9,... | collective-permute-start | bytes 2433032 | tf_op jit(solution)/shard_map/ppermute | solution.py:67
  6.5 20.3 %collective-permute-start = (bf16[528,768]{1,0:T(8,128)(2,1)}, bf16[528,768]{1,0:T(8,128)(2,1)S(1)}, u32[]{:S(2)}, u32[]{:S(2)}) collective-permute-start(bf16[528,768]{1,0:T(8,128)(2,1)} %get-tuple-element.7.refs_0_.refs_3_), channel_id=1, source_target_pairs={{0,4},{1,67},{2,6},{3,1},{4,8},{5,71},{6,10},{7,5},{8,12},{9,75},{... | collective-permute-start | bytes 2433032 | tf_op jit(solution)/shard_map/ppermute | solution.py:67
  9.3 17.6 %collective-permute-start.6 = (bf16[528,768]{1,0:T(8,128)(2,1)}, bf16[528,768]{1,0:T(8,128)(2,1)S(1)}, u32[]{:S(2)}, u32[]{:S(2)}) collective-permute-start(bf16[528,768]{1,0:T(8,128)(2,1)} %get-tuple-element.7.refs_0_.refs_3_), channel_id=1, source_target_pairs={{0,48},{1,17},{2,50},{3,19},{4,52},{5,21},{6,54},{7,23},{8,56},{9,... | collective-permute-start | bytes 2433032 | tf_op jit(solution)/shard_map/ppermute | solution.py:67
  9.3 20.4 %collective-permute-start.11 = (bf16[528,768]{1,0:T(8,128)(2,1)}, bf16[528,768]{1,0:T(8,128)(2,1)}, u32[]{:S(2)}, u32[]{:S(2)}) collective-permute-start(bf16[528,768]{1,0:T(8,128)(2,1)} %get-tuple-element.7.refs_0_.refs_3_), channel_id=1, source_target_pairs={{0,12},{1,3},{2,14},{3,65},{4,0},{5,7},{6,2},{7,69},{8,4},{9,11},{... | collective-permute-start | bytes 2433032 | tf_op jit(solution)/shard_map/ppermute | solution.py:67
  9.3 23.5 %collective-permute-start.16 = (bf16[528,768]{1,0:T(8,128)(2,1)}, bf16[528,768]{1,0:T(8,128)(2,1)}, u32[]{:S(2)}, u32[]{:S(2)}) collective-permute-start(bf16[528,768]{1,0:T(8,128)(2,1)} %get-tuple-element.7.refs_0_.refs_3_), channel_id=1, source_target_pairs={{0,1},{1,0},{2,3},{3,2},{4,5},{5,4},{6,7},{7,6},{8,9},{9,8},{10,11... | collective-permute-start | bytes 2433032 | tf_op jit(solution)/shard_map/ppermute | solution.py:71
  21.1 14.9 %collective-permute-start.9 = (bf16[528,768]{1,0:T(8,128)(2,1)S(1)}, bf16[528,768]{1,0:T(8,128)(2,1)S(1)}, u32[]{:S(2)}, u32[]{:S(2)}) collective-permute-start(bf16[528,768]{1,0:T(8,128)(2,1)S(1)} %collective-permute-done.8.refs_4_.refs_5_.refs_3_), channel_id=1, source_target_pairs={{0,2},{1,13},{2,64},{3,15},{4,6},{5,1},{6,68},{7,3},{8,10},{9,5},{... | collective-permute-start | bytes 2433032 | tf_op jit(solution)/shard_map/ppermute | solution.py:67
  26.8 18.6 %collective-permute-start.1 = (bf16[528,768]{1,0:T(8,128)(2,1)S(1)}, bf16[528,768]{1,0:T(8,128)(2,1)}, u32[]{:S(2)}, u32[]{:S(2)}) collective-permute-start(bf16[528,768]{1,0:T(8,128)(2,1)S(1)} %collective-permute-done.refs_3_.refs_4_), channel_id=1, source_target_pairs={{0,66},{1,5},{2,0},{3,7},{4,70},{5,9},{6,4},{7,11},{8,74},{9,13},{... | collective-permute-start | bytes 2433032 | tf_op jit(solution)/shard_map/ppermute | solution.py:67
  26.8 44.8 %copy-start.1 = (bf16[528,768]{1,0:T(8,128)(2,1)}, bf16[528,768]{1,0:T(8,128)(2,1)S(1)}, u32[]{:S(2)}) copy-start(bf16[528,768]{1,0:T(8,128)(2,1)S(1)} %collective-permute-done.6.refs_2_.refs_9_) | copy-start | bytes 2433028
  26.8 20.7 %collective-permute-start.4 = (bf16[528,768]{1,0:T(8,128)(2,1)S(1)}, bf16[528,768]{1,0:T(8,128)(2,1)}, u32[]{:S(2)}, u32[]{:S(2)}) collective-permute-start(bf16[528,768]{1,0:T(8,128)(2,1)S(1)} %collective-permute-done.refs_3_.refs_4_), channel_id=1, source_target_pairs={{0,4},{1,67},{2,6},{3,1},{4,8},{5,71},{6,10},{7,5},{8,12},{9,75},{... | collective-permute-start | bytes 2433032 | tf_op jit(solution)/shard_map/ppermute | solution.py:67
  29.6 21.1 %collective-permute-start.12 = (bf16[528,768]{1,0:T(8,128)(2,1)}, bf16[528,768]{1,0:T(8,128)(2,1)}, u32[]{:S(2)}, u32[]{:S(2)}) collective-permute-start(bf16[528,768]{1,0:T(8,128)(2,1)} %collective-permute-done.11.refs_1_.refs_5_.refs_6_), channel_id=1, source_target_pairs={{0,1},{1,0},{2,3},{3,2},{4,5},{5,4},{6,7},{7,6},{8,9},{9,8},{10,11... | collective-permute-start | bytes 2433032 | tf_op jit(solution)/shard_map/ppermute | solution.py:71
  30.2 0.7 copy-start.6
  30.2 0.7 copy-start.5
  31.0 0.7 copy-start.7
  32.2 18.6 %copy-start.4 = (pred[22]{0:T(512)(128)(4,1)S(1)}, pred[22]{0:T(512)(128)(4,1)}, u32[]{:S(2)}) copy-start(pred[22]{0:T(512)(128)(4,1)} %constant.116.clone) | copy-start | bytes 70
  32.8 33.8 %collective-permute-start.18 = (bf16[528,768]{1,0:T(8,128)(2,1)S(1)}, bf16[528,768]{1,0:T(8,128)(2,1)}, u32[]{:S(2)}, u32[]{:S(2)}) collective-permute-start(bf16[528,768]{1,0:T(8,128)(2,1)S(1)} %collective-permute-done.8.refs_4_.refs_5_.refs_3_), channel_id=1, source_target_pairs={{0,1},{1,0},{2,3},{3,2},{4,5},{5,4},{6,7},{7,6},{8,9},{9,8},{10,11... | collective-permute-start | bytes 2433032 | tf_op jit(solution)/shard_map/ppermute | solution.py:71
  36.0 35.7 %copy-start.2 = (bf16[528,768]{1,0:T(8,128)(2,1)}, bf16[528,768]{1,0:T(8,128)(2,1)S(1)}, u32[]{:S(2)}) copy-start(bf16[528,768]{1,0:T(8,128)(2,1)S(1)} %collective-permute-done.9.refs_1_.refs_8_.refs_4_) | copy-start | bytes 2433028
  36.0 32.5 %collective-permute-start.17 = (bf16[528,768]{1,0:T(8,128)(2,1)S(1)}, bf16[528,768]{1,0:T(8,128)(2,1)}, u32[]{:S(2)}, u32[]{:S(2)}) collective-permute-start(bf16[528,768]{1,0:T(8,128)(2,1)S(1)} %collective-permute-done.refs_3_.refs_4_), channel_id=1, source_target_pairs={{0,1},{1,0},{2,3},{3,2},{4,5},{5,4},{6,7},{7,6},{8,9},{9,8},{10,11... | collective-permute-start | bytes 2433032 | tf_op jit(solution)/shard_map/ppermute | solution.py:71
  45.5 22.5 %collective-permute-start.14 = (bf16[528,768]{1,0:T(8,128)(2,1)S(1)}, bf16[528,768]{1,0:T(8,128)(2,1)}, u32[]{:S(2)}, u32[]{:S(2)}) collective-permute-start(bf16[528,768]{1,0:T(8,128)(2,1)S(1)} %collective-permute-done.6.refs_2_.refs_9_), channel_id=1, source_target_pairs={{0,1},{1,0},{2,3},{3,2},{4,5},{5,4},{6,7},{7,6},{8,9},{9,8},{10,11... | collective-permute-start | bytes 2433032 | tf_op jit(solution)/shard_map/ppermute | solution.py:71
  47.5 23.6 %collective-permute-start.10 = (bf16[528,768]{1,0:T(8,128)(2,1)S(1)}, bf16[528,768]{1,0:T(8,128)(2,1)}, u32[]{:S(2)}, u32[]{:S(2)}) collective-permute-start(bf16[528,768]{1,0:T(8,128)(2,1)S(1)} %collective-permute-done.9.refs_1_.refs_8_.refs_4_), channel_id=1, source_target_pairs={{0,2},{1,13},{2,64},{3,15},{4,6},{5,1},{6,68},{7,3},{8,10},{9,5},{... | collective-permute-start | bytes 2433032 | tf_op jit(solution)/shard_map/ppermute | solution.py:67
  50.8 20.4 %collective-permute-start.19 = (bf16[528,768]{1,0:T(8,128)(2,1)S(1)}, bf16[528,768]{1,0:T(8,128)(2,1)}, u32[]{:S(2)}, u32[]{:S(2)}) collective-permute-start(bf16[528,768]{1,0:T(8,128)(2,1)S(1)} %collective-permute-done.9.refs_1_.refs_8_.refs_4_), channel_id=1, source_target_pairs={{0,1},{1,0},{2,3},{3,2},{4,5},{5,4},{6,7},{7,6},{8,9},{9,8},{10,11... | collective-permute-start | bytes 2433032 | tf_op jit(solution)/shard_map/ppermute | solution.py:71
  51.1 1.1 copy-start
  66.6 62.4 %collective-permute-start.7 = (bf16[528,768]{1,0:T(8,128)(2,1)S(1)}, bf16[528,768]{1,0:T(8,128)(2,1)S(1)}, u32[]{:S(2)}, u32[]{:S(2)}) collective-permute-start(bf16[528,768]{1,0:T(8,128)(2,1)S(1)} %collective-permute-done.6.refs_2_.refs_9_), channel_id=1, source_target_pairs={{0,12},{1,3},{2,14},{3,65},{4,0},{5,7},{6,2},{7,69},{8,4},{9,11},{... | collective-permute-start | bytes 2433032 | tf_op jit(solution)/shard_map/ppermute | solution.py:67
  67.9 27.5 %collective-permute-start.13 = (bf16[528,768]{1,0:T(8,128)(2,1)}, bf16[528,768]{1,0:T(8,128)(2,1)S(1)}, u32[]{:S(2)}, u32[]{:S(2)}) collective-permute-start(bf16[528,768]{1,0:T(8,128)(2,1)} %collective-permute-done.1.refs_0_.refs_7_), channel_id=1, source_target_pairs={{0,1},{1,0},{2,3},{3,2},{4,5},{5,4},{6,7},{7,6},{8,9},{9,8},{10,11... | collective-permute-start | bytes 2433032 | tf_op jit(solution)/shard_map/ppermute | solution.py:71
  68.5 27.0 %collective-permute-start.2 = (bf16[528,768]{1,0:T(8,128)(2,1)}, bf16[528,768]{1,0:T(8,128)(2,1)S(1)}, u32[]{:S(2)}, u32[]{:S(2)}) collective-permute-start(bf16[528,768]{1,0:T(8,128)(2,1)} %collective-permute-done.1.refs_0_.refs_7_), channel_id=1, source_target_pairs={{0,16},{1,49},{2,18},{3,51},{4,20},{5,53},{6,22},{7,55},{8,24},{9,... | collective-permute-start | bytes 2433032 | tf_op jit(solution)/shard_map/ppermute | solution.py:67
  71.1 27.7 %collective-permute-start.15 = (bf16[528,768]{1,0:T(8,128)(2,1)}, bf16[528,768]{1,0:T(8,128)(2,1)S(1)}, u32[]{:S(2)}, u32[]{:S(2)}) collective-permute-start(bf16[528,768]{1,0:T(8,128)(2,1)} %collective-permute-done.4.refs_2_), channel_id=1, source_target_pairs={{0,1},{1,0},{2,3},{3,2},{4,5},{5,4},{6,7},{7,6},{8,9},{9,8},{10,11... | collective-permute-start | bytes 2433032 | tf_op jit(solution)/shard_map/ppermute | solution.py:71
  71.2 27.7 %collective-permute-start.20 = (bf16[528,768]{1,0:T(8,128)(2,1)}, bf16[528,768]{1,0:T(8,128)(2,1)S(1)}, u32[]{:S(2)}, u32[]{:S(2)}) collective-permute-start(bf16[528,768]{1,0:T(8,128)(2,1)} %collective-permute-done.10.refs_0_.refs_5_), channel_id=1, source_target_pairs={{0,1},{1,0},{2,3},{3,2},{4,5},{5,4},{6,7},{7,6},{8,9},{9,8},{10,11... | collective-permute-start | bytes 2433032 | tf_op jit(solution)/shard_map/ppermute | solution.py:71
  95.4 33.6 %copy-start.3 = (bf16[528,768]{1,0:T(8,128)(2,1)S(1)}, bf16[528,768]{1,0:T(8,128)(2,1)}, u32[]{:S(2)}) copy-start(bf16[528,768]{1,0:T(8,128)(2,1)} %copy-done.2) | copy-start | bytes 2433028
  95.4 3.5 %copy-start.8 = (bf16[528,768]{1,0:T(8,128)(2,1)}, bf16[528,768]{1,0:T(8,128)(2,1)S(1)}, u32[]{:S(2)}) copy-start(bf16[528,768]{1,0:T(8,128)(2,1)S(1)} %collective-permute-done.13.refs_11_.refs_7_) | copy-start | bytes 2433028
  95.4 33.6 %collective-permute-start.5 = (bf16[528,768]{1,0:T(8,128)(2,1)}, bf16[528,768]{1,0:T(8,128)(2,1)S(1)}, u32[]{:S(2)}, u32[]{:S(2)}) collective-permute-start(bf16[528,768]{1,0:T(8,128)(2,1)} %collective-permute-done.4.refs_2_), channel_id=1, source_target_pairs={{0,48},{1,17},{2,50},{3,19},{4,52},{5,21},{6,54},{7,23},{8,56},{9,... | collective-permute-start | bytes 2433032 | tf_op jit(solution)/shard_map/ppermute | solution.py:67
  95.5 33.5 %collective-permute-start.3 = (bf16[528,768]{1,0:T(8,128)(2,1)S(1)}, bf16[528,768]{1,0:T(8,128)(2,1)S(1)}, u32[]{:S(2)}, u32[]{:S(2)}) collective-permute-start(bf16[528,768]{1,0:T(8,128)(2,1)S(1)} %collective-permute-done.2.refs_1_), channel_id=1, source_target_pairs={{0,4},{1,67},{2,6},{3,1},{4,8},{5,71},{6,10},{7,5},{8,12},{9,75},{... | collective-permute-start | bytes 2433032 | tf_op jit(solution)/shard_map/ppermute | solution.py:67
  98.9 1.0 copy-start.9
  99.8 0.9 copy-start.10

commit v3 on v2

v3 whole, which is shorter than its diff:
```python
import functools

import jax
import jax.numpy as jnp
import numpy as np
from jax import lax
from jax.experimental import pallas as pl
from jax.experimental.pallas import tpu as pltpu
from jax.sharding import PartitionSpec as P

D = 768
RB = 512
GROUPS = 8
META = 16
SENT = RB + META
UNROLL = 4
ABSENT = -4.0
LOW = -1e30
AXES = ("group", "row")

UNIT = ((1, 0, 0), (0, 1, 0), (0, 0, 1), (3, 0, 0), (0, 3, 0), (0, 0, 3))
PARENT = (None,) + (0, 0, 0, 2, 1, 3, 6, 4, 4, 5, 5, 7)
DIRS = (
    (None,) + (5, 0, 2, 1, 3, 4, 0, 5, 1, 5, 2, 0),
    (None,) + (4, 3, 1, 2, 0, 5, 3, 4, 2, 4, 1, 3),
)
SLOTS = len(PARENT)
OTHER = 20
MEETINGS = (
    ((0, (0, 20)), (1, (0, 20, 21)), (2, (0, 1, 20, 21)), (3, (1, 2, 20, 21))),
    (
        (4, (0, 1, 2, 3, 21, 22)),
        (5, (2, 3, 4, 20, 21, 23, 24, 25)),
        (6, (0, 1, 4, 5, 20, 22, 23, 25, 26)),
    ),
    (
        (7, (0, 3, 4, 5, 21, 22, 23, 24, 26, 27)),
        (8, (3, 5, 6, 7, 20, 21, 24, 25, 27)),
        (9, (0, 1, 2, 5, 6, 8, 22, 26, 27)),
    ),
    ((10, (2, 9, 20, 21, 23)), (11, (2, 8, 9, 20, 26)), (12, (23, 27))),
)


def members(meeting):
    rows = tuple(k for k, partners in meeting)
    rest = sorted({k for row, partners in meeting for k in partners} - set(rows))
    return rows, rows + tuple(rest)


NAMES = tuple(sorted({k for meeting in MEETINGS for k in members(meeting)[1]}))


def offsets():
    table = []
    for core in range(2):
        held = [(0, 0, 0)]
        for i in range(1, SLOTS):
            step, base = UNIT[DIRS[core][i]], held[PARENT[i]]
            held.append(tuple((a + b) % 4 for a, b in zip(step, base)))
        table.append(held)
    return table


def place(x, y, z, core):
    group = (y // 2) * 4 + x
    row = (z * 2 + y % 2) * 2 + core
    return group * 16 + row


def fetch(block, steps):
    pairs = []
    for x in range(4):
        for y in range(4):
            for z in range(4):
                for core in range(2):
                    dx, dy, dz = steps[core]
                    source = place((x + dx) % 4, (y + dy) % 4, (z + dz) % 4, core)
                    pairs.append((source, place(x, y, z, core)))
    return lax.ppermute(block, AXES, sorted(pairs))


def flip(block):
    return lax.ppermute(block, AXES, [(i, i ^ 1) for i in range(128)])


def prepare_kernel(embeds_ref, member_ref, block_ref, target_ref):
    member = member_ref[...].astype(jnp.float32)
    column = jnp.transpose(jnp.broadcast_to(member, (128, RB)))[:, 0:1]
    above = lax.broadcasted_iota(jnp.int32, (RB, RB), 0)
    across = lax.broadcasted_iota(jnp.int32, (RB, RB), 1)
    before = (column < member) | ((column == member) & (above < across))
    target = jnp.sum(before.astype(jnp.float32), axis=0, keepdims=True).astype(jnp.int32)
    target_ref[...] = target
    values = embeds_ref[...].astype(jnp.float32)
    total = jnp.sum(values * values, axis=1, keepdims=True)
    normed = (values * lax.rsqrt(total + 1e-06)).astype(jnp.bfloat16)
    placer = (above == target).astype(jnp.bfloat16)
    block_ref[0:RB, :] = jnp.dot(placer, normed, preferred_element_type=jnp.float32).astype(
        jnp.bfloat16
    )
    ordered = jnp.sum(jnp.where(above == target, member, 0.0), axis=1, keepdims=True)
    ordered = jnp.transpose(jnp.broadcast_to(ordered, (RB, 128)))[0:META]
    block_ref[RB:SENT, :] = jnp.zeros((META, D), jnp.bfloat16)
    block_ref[RB:SENT, 0:RB] = ordered.astype(jnp.bfloat16)


def prepare(embeds, member):
    return pl.pallas_call(
        prepare_kernel,
        out_shape=(
            jax.ShapeDtypeStruct((SENT, D), jnp.bfloat16),
            jax.ShapeDtypeStruct((1, RB), jnp.int32),
        ),
        name="prepare",
    )(embeds, member.reshape(1, RB))


def meet_kernel(total, rows, pairs, itself, lists, table, *refs):
    blocks, refs = refs[:total], refs[total:]
    if lists:
        where_ref, refs = refs[0], refs[1:]
        before, refs = refs[: len(lists) - 1], refs[len(lists) - 1 :]
    out_ref, held, across, down, row_best, column_best, sems = refs
    copies = []
    for k in range(total):
        copies.append(pltpu.make_async_copy(blocks[k], held.at[k], sems.at[k]))
        copies[k].start()
    row_best[...] = jnp.full_like(row_best, LOW)
    column_best[...] = jnp.full_like(column_best, LOW)
    if lists:
        out_ref[...] = jnp.full_like(out_ref, ABSENT)
    for k in range(total):
        copies[k].wait()
        clusters = held[k, RB:SENT, 0:RB].astype(jnp.float32)[0:8]
        across[k] = clusters
        if k < rows:
            down[k] = jnp.transpose(jnp.broadcast_to(clusters[0:1], (128, RB)))

    def meet(i, j, same):
        scores = lax.dot_general(
            held[i, 0:RB, :],
            held[j, 0:RB, :],
            (((1,), (1,)), ((), ())),
            preferred_element_type=jnp.float32,
        )
        keep = jnp.concatenate([down[i]] * (RB // 128), axis=1) == across[j, 0:1, :]
        if same:
            one = lax.broadcasted_iota(jnp.int32, (RB, RB), 0)
            keep = keep & (one != lax.broadcasted_iota(jnp.int32, (RB, RB), 1))
        scores = jnp.where(keep, scores, LOW)
        most = scores[:, 0:128]
        for q in range(1, RB // 128):
            most = jnp.maximum(most, scores[:, 128 * q : 128 * q + 128])
        row_best[i] = jnp.maximum(row_best[i], most)
        top = jnp.max(scores.reshape(RB // 8, 8, RB), axis=0)
        column_best[j] = jnp.maximum(column_best[j], top)

    if itself:
        meet(0, 0, True)

    def some(step, carry):
        for u in range(UNROLL):
            p = step * UNROLL + u
            meet(table[0, p], table[1, p], False)
        return carry

    lax.fori_loop(0, pairs // UNROLL, some, 0)
    for p in range(pairs // UNROLL * UNROLL, pairs):
        meet(table[0, p], table[1, p], False)

    def found_in(k):
        found = jnp.max(column_best[k], axis=0, keepdims=True)
        if k < rows:
            turned = jnp.transpose(row_best[k])
            found = jnp.maximum(found, jnp.max(turned, axis=0, keepdims=True))
        return found

    if not lists:
        for k in range(total):
            out_ref[k : k + 1, :] = found_in(k)
        return
    for number, name in enumerate(NAMES):
        found = jnp.full((1, RB), ABSENT, jnp.float32)
        if name in lists[0]:
            found = jnp.maximum(found, found_in(lists[0].index(name)))
        for ref, names in zip(before, lists[1:]):
            if name in names:
                at = names.index(name)
                found = jnp.maximum(found, ref[at : at + 1, :])
        out_ref[where_ref[number]] = found


def meet(held, meeting, lists=(), where=None, before=()):
    rows, names = members(meeting)
    pairs = [(i, j) for i, partners in meeting for j in partners]
    itself = (0, 0) in pairs
    pairs = [(names.index(i), names.index(j)) for i, j in pairs if i != j]
    total = len(names)
    shape = (128, 1, RB) if lists else (total, RB)
    in_specs = [pl.BlockSpec(memory_space=pltpu.SMEM)]
    in_specs += [pl.BlockSpec(memory_space=pl.ANY)] * total
    if lists:
        in_specs += [pl.BlockSpec(memory_space=pltpu.SMEM)]
        in_specs += [pl.BlockSpec(memory_space=pltpu.VMEM)] * len(before)
    return pl.pallas_call(
        functools.partial(meet_kernel, total, len(rows), len(pairs), itself, lists),
        out_shape=jax.ShapeDtypeStruct(shape, jnp.float32),
        in_specs=in_specs,
        scratch_shapes=[
            pltpu.VMEM((total, SENT, D), jnp.bfloat16),
            pltpu.VMEM((total, 8, RB), jnp.float32),
            pltpu.VMEM((len(rows), RB, 128), jnp.float32),
            pltpu.VMEM((len(rows), RB, 128), jnp.float32),
            pltpu.VMEM((total, 8, RB), jnp.float32),
            pltpu.SemaphoreType.DMA((total,)),
        ],
        compiler_params=pltpu.CompilerParams(vmem_limit_bytes=40 * 2**20),
        cost_estimate=pl.CostEstimate(
            flops=2 * RB * RB * D * len(pairs),
            bytes_accessed=total * SENT * D * 2,
            transcendentals=0,
        ),
        name=f"meet_{len(pairs)}",
    )(
        jnp.asarray(np.array(pairs, np.int32).T),
        *[held[k] for k in names],
        *(() if where is None else (where,)),
        *before,
    )


def finish_kernel(arrived_ref, target_ref, out_ref):
    best = jnp.max(arrived_ref[...], axis=0, keepdims=True)
    column = jnp.transpose(jnp.broadcast_to(best, (128, RB)))[:, 0:1]
    above = lax.broadcasted_iota(jnp.int32, (RB, RB), 0)
    picked = jnp.where(above == target_ref[...], column, LOW)
    out_ref[...] = jnp.max(picked, axis=0, keepdims=True)


def finish(arrived, target):
    return pl.pallas_call(
        finish_kernel, out_shape=jax.ShapeDtypeStruct((1, RB), jnp.float32), name="finish"
    )(arrived, target)


def homes():
    group, row = lax.axis_index("group"), lax.axis_index("row")
    x, y, z, core = group % 4, (group // 4) * 2 + (row // 2) % 2, row // 4, row % 2
    table = jnp.array(offsets(), jnp.int32)
    own = jnp.where(core == 0, table[0], table[1])
    other = jnp.where(core == 0, table[1], table[0])
    names = np.array(NAMES)
    steps = jnp.where((names < OTHER)[:, None], own[names % OTHER], other[names % OTHER])
    cores = jnp.where(names < OTHER, core, 1 - core)
    at = place((x + steps[:, 0]) % 4, (y + steps[:, 1]) % 4, (z + steps[:, 2]) % 4, cores)
    return at.astype(jnp.int32)


def on_device(embeds, member):
    block, target = prepare(embeds, member)
    held = {0: block}
    for i in range(1, SLOTS):
        held[i] = fetch(held[PARENT[i]], (UNIT[DIRS[0][i]], UNIT[DIRS[1][i]]))
    for name in NAMES:
        if name >= OTHER:
            held[name] = flip(held[name - OTHER])
    before = [meet(held, meeting) for meeting in MEETINGS[:-1]]
    lists = tuple(members(meeting)[1] for meeting in (MEETINGS[-1],) + MEETINGS[:-1])
    outgoing = meet(held, MEETINGS[-1], lists, homes(), before)
    arrived = lax.all_to_all(outgoing, AXES, split_axis=0, concat_axis=0, tiled=True)
    return finish(arrived.reshape(128, RB), target).reshape(-1)


def solution(mesh):
    in_specs = (P(AXES, None), P(AXES))
    return jax.shard_map(
        on_device, mesh=mesh, in_specs=in_specs, out_specs=P(AXES), check_vma=False
    )
```

time: 171 us -> 128 us (0.75)
  Pallas kernels: 93.4 us -> 55.1 us
  waiting for transfers between devices: 19.3 us -> 11.7 us
  starting transfers between devices: 34.1 us -> 36.9 us
    pallas_call x4, Pallas kernels: 88.3 us -> 50.2 us  [meet(): pl.pallas_call(functools.partial(meet_kernel, total, len(rows), len(pairs...]
    ppermute x9 -> x8, starting transfers between devices: 8.91 us -> 19.6 us  [flip(): return lax.ppermute(block, AXES, [(i, i ^ 1) for i in range(128)])]
    ppermute x12, starting transfers between devices: 25.2 us -> 17.3 us  [fetch(): return lax.ppermute(block, AXES, sorted(pairs))]
    ppermute x12, waiting for transfers between devices: 19.3 us -> 11.7 us  [fetch(): return lax.ppermute(block, AXES, sorted(pairs))]
  transfers between devices with their start and end apart: 21 -> 20, of which waited for: 3 -> 5; matrix products, arithmetic and copies ran while one was open for 1% -> 1% of each run, Pallas kernels for 39% -> 32%
where the time goes in v3:
time: 128 us
  Pallas kernels  55.1 us (43%)
  starting transfers between devices  36.9 us (29%)
  blocking collectives  16.7 us (13%)
  waiting for transfers between devices  11.7 us (9%)
  local copies, waits for them, and re-layouts  7.13 us (6%)
    pallas_call x4, Pallas kernels, meet(): pl.pallas_call(functools.partial(meet_kernel, total, len(rows), len(pairs...  50.2 us
    ppermute x8, starting transfers between devices, flip(): return lax.ppermute(block, AXES, [(i, i ^ 1) for i in range(128)])  19.6 us
    ppermute x12, starting transfers between devices, fetch(): return lax.ppermute(block, AXES, sorted(pairs))  17.3 us
    all_to_all x1, blocking collectives, on_device(): lax.all_to_all(outgoing, AXES, split_axis=0, concat_axis=0, tiled=True)  16.7 us
    ppermute x12, waiting for transfers between devices, fetch(): return lax.ppermute(block, AXES, sorted(pairs))  11.7 us
    unnamed x23, local copies, waits for them, and re-layouts  5.81 us
    pallas_call x1, Pallas kernels, prepare(): pl.pallas_call(prepare_kernel, out_shape=(jax.ShapeDtypeStruct((SENT, D),...  3.11 us
  transfers between devices with their start and end apart: 20, of which 5 were waited for; matrix products, arithmetic and copies ran while one was open for 1% of the time, Pallas kernels for 32%

profile of v3, /device:TPU:1, one launch (start us, length us, event | category | flops | bytes accessed | tf_op | source)
XLA Modules:
  0.0 128.0 jit_solution(7802886418603453214)
XLA Ops:
  0.0 3.1 %prepare.1 = (bf16[528,768]{1,0:T(8,128)(2,1)}, s32[1,512]{1,0:T(1,128)}) custom-call(bf16[512,768]{1,0:T(8,128)(2,1)} %embeds_ref.1, s32[1,512]{1,0:T(1,128)} %bitcast.10), custom_call_target="tpu_custom_call" | custom-call | tf_op jit(solution)/shard_map/prepare/pallas_call | solution.py:109
  3.1 3.6 %collective-permute-start.4 = (bf16[528,768]{1,0:T(8,128)(2,1)}, bf16[528,768]{1,0:T(8,128)(2,1)S(1)}, u32[]{:S(2)}, u32[]{:S(2)}) collective-permute-start(bf16[528,768]{1,0:T(8,128)(2,1)} %get-tuple-element.7.refs_0_.refs_3_), channel_id=1, source_target_pairs={{0,12},{1,67},{2,14},{3,1},{4,0},{5,71},{6,2},{7,5},{8,4},{9,75},{... | collective-permute-start | bytes 2433032 | tf_op jit(solution)/shard_map/ppermute | solution.py:80
  6.7 1.2 collective-permute-start.8
  7.9 0.0 collective-permute-start
  7.9 3.5 %collective-permute-start.12 = (bf16[528,768]{1,0:T(8,128)(2,1)}, bf16[528,768]{1,0:T(8,128)(2,1)S(1)}, u32[]{:S(2)}, u32[]{:S(2)}) collective-permute-start(bf16[528,768]{1,0:T(8,128)(2,1)} %get-tuple-element.7.refs_0_.refs_3_), channel_id=1, source_target_pairs={{0,1},{1,0},{2,3},{3,2},{4,5},{5,4},{6,7},{7,6},{8,9},{9,8},{10,11... | collective-permute-start | bytes 2433032 | tf_op jit(solution)/shard_map/ppermute | solution.py:84
  11.4 4.8 %collective-permute-done.4.refs_3_.refs_6_ = bf16[528,768]{1,0:T(8,128)(2,1)S(1)} collective-permute-done((bf16[528,768]{1,0:T(8,128)(2,1)}, bf16[528,768]{1,0:T(8,128)(2,1)S(1)}, u32[]{:S(2)}, u32[]{:S(2)}) %collective-permute-start.4) | collective-permute-done | bytes 811040 | tf_op jit(solution)/shard_map/ppermute | solution.py:80
  16.2 1.6 %collective-permute-start.5 = (bf16[528,768]{1,0:T(8,128)(2,1)S(1)}, bf16[528,768]{1,0:T(8,128)(2,1)}, u32[]{:S(2)}, u32[]{:S(2)}) collective-permute-start(bf16[528,768]{1,0:T(8,128)(2,1)S(1)} %collective-permute-done.4.refs_3_.refs_6_), channel_id=1, source_target_pairs={{0,2},{1,5},{2,64},{3,7},{4,6},{5,9},{6,68},{7,11},{8,10},{9,13},{... | collective-permute-start | bytes 2433032 | tf_op jit(solution)/shard_map/ppermute | solution.py:80
  17.8 1.7 %collective-permute-done.8.refs_2_.refs_5_.refs_3_ = bf16[528,768]{1,0:T(8,128)(2,1)S(1)} collective-permute-done((bf16[528,768]{1,0:T(8,128)(2,1)}, bf16[528,768]{1,0:T(8,128)(2,1)S(1)}, u32[]{:S(2)}, u32[]{:S(2)}) %collective-permute-start.8) | collective-permute-done | bytes 811040 | tf_op jit(solution)/shard_map/ppermute | solution.py:80
  19.5 3.5 %collective-permute-start.9 = (bf16[528,768]{1,0:T(8,128)(2,1)S(1)}, bf16[528,768]{1,0:T(8,128)(2,1)}, u32[]{:S(2)}, u32[]{:S(2)}) collective-permute-start(bf16[528,768]{1,0:T(8,128)(2,1)S(1)} %collective-permute-done.8.refs_2_.refs_5_.refs_3_), channel_id=1, source_target_pairs={{0,66},{1,13},{2,0},{3,15},{4,70},{5,1},{6,4},{7,3},{8,74},{9,5},{... | collective-permute-start | bytes 2433032 | tf_op jit(solution)/shard_map/ppermute | solution.py:80
  23.0 0.0 collective-permute-done.refs_1_.refs_4_
  23.0 1.6 %collective-permute-start.1 = (bf16[528,768]{1,0:T(8,128)(2,1)S(1)}, bf16[528,768]{1,0:T(8,128)(2,1)}, u32[]{:S(2)}, u32[]{:S(2)}) collective-permute-start(bf16[528,768]{1,0:T(8,128)(2,1)S(1)} %collective-permute-done.refs_1_.refs_4_), channel_id=1, source_target_pairs={{0,16},{1,49},{2,18},{3,51},{4,20},{5,53},{6,22},{7,55},{8,24},{9,... | collective-permute-start | bytes 2433032 | tf_op jit(solution)/shard_map/ppermute | solution.py:80
  24.5 4.0 %collective-permute-start.13 = (bf16[528,768]{1,0:T(8,128)(2,1)S(1)}, bf16[528,768]{1,0:T(8,128)(2,1)}, u32[]{:S(2)}, u32[]{:S(2)}) collective-permute-start(bf16[528,768]{1,0:T(8,128)(2,1)S(1)} %collective-permute-done.refs_1_.refs_4_), channel_id=1, source_target_pairs={{0,1},{1,0},{2,3},{3,2},{4,5},{5,4},{6,7},{7,6},{8,9},{9,8},{10,11... | collective-permute-start | bytes 2433032 | tf_op jit(solution)/shard_map/ppermute | solution.py:84
  28.5 0.0 collective-permute-done.12.refs_4_.refs_7_.refs_10_.refs_6_
  28.5 0.1 collective-permute-start.14
  28.6 0.7 copy-done.9
  29.3 0.0 copy-done.8
  29.3 0.1 copy.20
  29.4 0.1 copy.21
  29.5 0.6 copy-done.10
  30.1 0.6 gather_fusion
  30.6 0.0 copy-start.7
  30.7 0.6 gather_fusion.1
  31.2 2.3 %collective-permute-done.5.refs_2_.refs_9_ = bf16[528,768]{1,0:T(8,128)(2,1)} collective-permute-done((bf16[528,768]{1,0:T(8,128)(2,1)S(1)}, bf16[528,768]{1,0:T(8,128)(2,1)}, u32[]{:S(2)}, u32[]{:S(2)}) %collective-permute-start.5) | collective-permute-done | bytes 811040 | tf_op jit(solution)/shard_map/ppermute | solution.py:80
  33.5 0.0 collective-permute-start.17
  33.5 0.0 collective-permute-done.9.refs_0_.refs_7_
  33.5 0.0 collective-permute-start.6
  33.5 0.9 collective-permute-done.1.refs_1_.refs_8_
  34.5 11.5 %collective-permute-start.15 = (bf16[528,768]{1,0:T(8,128)(2,1)}, bf16[528,768]{1,0:T(8,128)(2,1)}, u32[]{:S(2)}, u32[]{:S(2)}) collective-permute-start(bf16[528,768]{1,0:T(8,128)(2,1)} %collective-permute-done.5.refs_2_.refs_9_), channel_id=1, source_target_pairs={{0,1},{1,0},{2,3},{3,2},{4,5},{5,4},{6,7},{7,6},{8,9},{9,8},{10,11... | collective-permute-start | bytes 2433032 | tf_op jit(solution)/shard_map/ppermute | solution.py:84
  46.0 0.0 collective-permute-done.13.refs_5_.refs_8_.refs_11_.refs_7_
  46.0 0.0 collective-permute-start.18
  46.0 0.0 collective-permute-done.14.refs_10_.refs_13_.refs_8_
  46.0 0.5 collective-permute-start.19
  46.5 0.1 broadcast_select_fusion
  46.6 0.2 fusion.2
  46.8 0.6 copy-done.6
  47.5 1.1 copy-done
  48.6 8.7 %meet_12.2.refs_12_ = f32[6,512]{1,0:T(8,128)S(1)} custom-call(s32[2,12]{1,0:T(2,128)S(1)} %copy-done.6, bf16[528,768]{1,0:T(8,128)(2,1)S(1)} %copy-done, bf16[528,768]{1,0:T(8,128)(2,1)S(1)} %collective-permute-done.refs_1_.refs_4_, bf16[528,768]{1,0:T(8,128)(2,1)S(1)} %collective-permute-done.8.refs_2_.refs_5_.refs_3_, ...), custom_call_target="tpu_custom_call" | custom-call | flops 4831838208 | bytes 4866048 | tf_op jit(solution)/shard_map/meet_12/pallas_call | solution.py:206
  57.3 0.0 copy-start.4
  57.4 0.0 collective-permute-done.17.refs_9_.refs_12_
  57.4 3.0 %collective-permute-start.10 = (bf16[528,768]{1,0:T(8,128)(2,1)}, bf16[528,768]{1,0:T(8,128)(2,1)S(1)}, u32[]{:S(2)}, u32[]{:S(2)}) collective-permute-start(bf16[528,768]{1,0:T(8,128)(2,1)} %collective-permute-done.9.refs_0_.refs_7_), channel_id=1, source_target_pairs={{0,4},{1,3},{2,6},{3,65},{4,8},{5,7},{6,10},{7,69},{8,12},{9,11},{... | collective-permute-start | bytes 2433032 | tf_op jit(solution)/shard_map/ppermute | solution.py:80
  60.3 0.0 collective-permute-done.6.refs_0_
  60.3 0.0 collective-permute-start.11
  60.3 0.0 collective-permute-done.18.refs_11_.refs_14_
  60.3 1.4 %collective-permute-start.2 = (bf16[528,768]{1,0:T(8,128)(2,1)}, bf16[528,768]{1,0:T(8,128)(2,1)S(1)}, u32[]{:S(2)}, u32[]{:S(2)}) collective-permute-start(bf16[528,768]{1,0:T(8,128)(2,1)} %collective-permute-done.1.refs_1_.refs_8_), channel_id=1, source_target_pairs={{0,4},{1,3},{2,6},{3,65},{4,8},{5,7},{6,10},{7,69},{8,12},{9,11},{... | collective-permute-start | bytes 2433032 | tf_op jit(solution)/shard_map/ppermute | solution.py:80
  61.7 0.0 collective-permute-done.15.refs_13_.refs_16_.refs_9_
  61.7 1.4 %collective-permute-start.3 = (bf16[528,768]{1,0:T(8,128)(2,1)}, bf16[528,768]{1,0:T(8,128)(2,1)S(1)}, u32[]{:S(2)}, u32[]{:S(2)}) collective-permute-start(bf16[528,768]{1,0:T(8,128)(2,1)} %collective-permute-done.1.refs_1_.refs_8_), channel_id=1, source_target_pairs={{0,12},{1,67},{2,14},{3,1},{4,0},{5,71},{6,2},{7,5},{8,4},{9,75},{... | collective-permute-start | bytes 2433032 | tf_op jit(solution)/shard_map/ppermute | solution.py:80
  63.1 0.0 collective-permute-done.19.refs_12_.refs_15_
  63.1 0.0 collective-permute-start.16
  63.1 14.9 %meet_23.1.refs_13_ = f32[14,512]{1,0:T(8,128)S(1)} custom-call(s32[2,23]{1,0:T(2,128)S(1)} %copy-done.5, bf16[528,768]{1,0:T(8,128)(2,1)} %collective-permute-done.9.refs_0_.refs_7_, bf16[528,768]{1,0:T(8,128)(2,1)} %collective-permute-done.1.refs_1_.refs_8_, bf16[528,768]{1,0:T(8,128)(2,1)} %collective-permute-done.5.refs_2_.refs_9_, ...), custom_call_target="tpu_custom_call" | custom-call | flops 9261023232 | bytes 11354112 | tf_op jit(solution)/shard_map/meet_23/pallas_call | solution.py:206
  78.0 0.0 copy-start.3
  78.0 0.0 collective-permute-done.10.refs_1_.refs_4_
  78.0 0.1 collective-permute-start.7
  78.1 2.0 %collective-permute-done.11.refs_2_.refs_5_ = bf16[528,768]{1,0:T(8,128)(2,1)S(1)} collective-permute-done((bf16[528,768]{1,0:T(8,128)(2,1)}, bf16[528,768]{1,0:T(8,128)(2,1)S(1)}, u32[]{:S(2)}, u32[]{:S(2)}) %collective-permute-start.11) | collective-permute-done | bytes 811040 | tf_op jit(solution)/shard_map/ppermute | solution.py:80
  80.0 0.0 collective-permute-done.16.refs_17_.refs_10_
  80.0 0.9 copy-done.1
  80.9 17.9 %meet_28.1.refs_14_ = f32[18,512]{1,0:T(8,128)S(1)} custom-call(s32[2,28]{1,0:T(2,128)S(1)} %copy-done.4, bf16[528,768]{1,0:T(8,128)(2,1)} %collective-permute-done.6.refs_0_, bf16[528,768]{1,0:T(8,128)(2,1)S(1)} %collective-permute-done.10.refs_1_.refs_4_, bf16[528,768]{1,0:T(8,128)(2,1)S(1)} %collective-permute-done.11.refs_2_.refs_5_, ...), custom_call_target="tpu_custom_call" | custom-call | flops 11274289152 | bytes 14598144 | tf_op jit(solution)/shard_map/meet_28/pallas_call | solution.py:206
  98.8 0.0 collective-permute-done.2.refs_0_
  98.8 0.0 collective-permute-done.3.refs_1_
  98.8 0.0 collective-permute-done.7.refs_2_
  98.9 1.1 copy-done.2
  100.0 8.7 %meet_12.3 = f32[128,1,512]{2,1,0:T(1,128)S(1)} custom-call(s32[2,12]{1,0:T(2,128)S(1)} %copy-done.3, bf16[528,768]{1,0:T(8,128)(2,1)S(1)} %collective-permute-done.2.refs_0_, bf16[528,768]{1,0:T(8,128)(2,1)S(1)} %collective-permute-done.3.refs_1_, bf16[528,768]{1,0:T(8,128)(2,1)S(1)} %collective-permute-done.7.refs_2_, ...), custom_call_target="tpu_custom_call" | custom-call | flops 4831838208 | bytes 8921088 | tf_op jit(solution)/shard_map/meet_12/pallas_call | solution.py:206
  108.7 16.7 %all_to_all.5 = f32[128,1,512]{2,1,0:T(1,128)S(1)} all-to-all(f32[128,1,512]{2,1,0:T(1,128)S(1)} %meet_12.3), channel_id=1, replica_groups=mesh['group'=8,'row'=16] {'group','row'}, dimensions={0} | all-to-all | bytes 524288 | tf_op jit(solution)/shard_map/all_to_all | solution.py:271
  125.4 0.7 copy.24
  126.1 1.9 %finish.1 = f32[1,512]{1,0:T(1,128)} custom-call(f32[128,512]{1,0:T(8,128)} %bitcast.9, s32[1,512]{1,0:T(1,128)} %get-tuple-element.8.target_ref), custom_call_target="tpu_custom_call" | custom-call | tf_op jit(solution)/shard_map/finish/pallas_call | solution.py:242
  (15 shorter events, 0.1 us)
Async XLA Ops:
  3.1 13.1 %collective-permute-start.4 = (bf16[528,768]{1,0:T(8,128)(2,1)}, bf16[528,768]{1,0:T(8,128)(2,1)S(1)}, u32[]{:S(2)}, u32[]{:S(2)}) collective-permute-start(bf16[528,768]{1,0:T(8,128)(2,1)} %get-tuple-element.7.refs_0_.refs_3_), channel_id=1, source_target_pairs={{0,12},{1,67},{2,14},{3,1},{4,0},{5,71},{6,2},{7,5},{8,4},{9,75},{... | collective-permute-start | bytes 2433032 | tf_op jit(solution)/shard_map/ppermute | solution.py:80
  6.7 12.8 %collective-permute-start.8 = (bf16[528,768]{1,0:T(8,128)(2,1)}, bf16[528,768]{1,0:T(8,128)(2,1)S(1)}, u32[]{:S(2)}, u32[]{:S(2)}) collective-permute-start(bf16[528,768]{1,0:T(8,128)(2,1)} %get-tuple-element.7.refs_0_.refs_3_), channel_id=1, source_target_pairs={{0,48},{1,17},{2,50},{3,19},{4,52},{5,21},{6,54},{7,23},{8,56},{9,... | collective-permute-start | bytes 2433032 | tf_op jit(solution)/shard_map/ppermute | solution.py:80
  7.9 15.1 %collective-permute-start = (bf16[528,768]{1,0:T(8,128)(2,1)}, bf16[528,768]{1,0:T(8,128)(2,1)S(1)}, u32[]{:S(2)}, u32[]{:S(2)}) collective-permute-start(bf16[528,768]{1,0:T(8,128)(2,1)} %get-tuple-element.7.refs_0_.refs_3_), channel_id=1, source_target_pairs={{0,4},{1,3},{2,6},{3,65},{4,8},{5,7},{6,10},{7,69},{8,12},{9,11},{... | collective-permute-start | bytes 2433032 | tf_op jit(solution)/shard_map/ppermute | solution.py:80
  7.9 20.6 %collective-permute-start.12 = (bf16[528,768]{1,0:T(8,128)(2,1)}, bf16[528,768]{1,0:T(8,128)(2,1)S(1)}, u32[]{:S(2)}, u32[]{:S(2)}) collective-permute-start(bf16[528,768]{1,0:T(8,128)(2,1)} %get-tuple-element.7.refs_0_.refs_3_), channel_id=1, source_target_pairs={{0,1},{1,0},{2,3},{3,2},{4,5},{5,4},{6,7},{7,6},{8,9},{9,8},{10,11... | collective-permute-start | bytes 2433032 | tf_op jit(solution)/shard_map/ppermute | solution.py:84
  16.2 17.3 %collective-permute-start.5 = (bf16[528,768]{1,0:T(8,128)(2,1)S(1)}, bf16[528,768]{1,0:T(8,128)(2,1)}, u32[]{:S(2)}, u32[]{:S(2)}) collective-permute-start(bf16[528,768]{1,0:T(8,128)(2,1)S(1)} %collective-permute-done.4.refs_3_.refs_6_), channel_id=1, source_target_pairs={{0,2},{1,5},{2,64},{3,7},{4,6},{5,9},{6,68},{7,11},{8,10},{9,13},{... | collective-permute-start | bytes 2433032 | tf_op jit(solution)/shard_map/ppermute | solution.py:80
  19.5 14.0 %collective-permute-start.9 = (bf16[528,768]{1,0:T(8,128)(2,1)S(1)}, bf16[528,768]{1,0:T(8,128)(2,1)}, u32[]{:S(2)}, u32[]{:S(2)}) collective-permute-start(bf16[528,768]{1,0:T(8,128)(2,1)S(1)} %collective-permute-done.8.refs_2_.refs_5_.refs_3_), channel_id=1, source_target_pairs={{0,66},{1,13},{2,0},{3,15},{4,70},{5,1},{6,4},{7,3},{8,74},{9,5},{... | collective-permute-start | bytes 2433032 | tf_op jit(solution)/shard_map/ppermute | solution.py:80
  23.0 11.5 %collective-permute-start.1 = (bf16[528,768]{1,0:T(8,128)(2,1)S(1)}, bf16[528,768]{1,0:T(8,128)(2,1)}, u32[]{:S(2)}, u32[]{:S(2)}) collective-permute-start(bf16[528,768]{1,0:T(8,128)(2,1)S(1)} %collective-permute-done.refs_1_.refs_4_), channel_id=1, source_target_pairs={{0,16},{1,49},{2,18},{3,51},{4,20},{5,53},{6,22},{7,55},{8,24},{9,... | collective-permute-start | bytes 2433032 | tf_op jit(solution)/shard_map/ppermute | solution.py:80
  24.5 21.5 %collective-permute-start.13 = (bf16[528,768]{1,0:T(8,128)(2,1)S(1)}, bf16[528,768]{1,0:T(8,128)(2,1)}, u32[]{:S(2)}, u32[]{:S(2)}) collective-permute-start(bf16[528,768]{1,0:T(8,128)(2,1)S(1)} %collective-permute-done.refs_1_.refs_4_), channel_id=1, source_target_pairs={{0,1},{1,0},{2,3},{3,2},{4,5},{5,4},{6,7},{7,6},{8,9},{9,8},{10,11... | collective-permute-start | bytes 2433032 | tf_op jit(solution)/shard_map/ppermute | solution.py:84
  28.5 17.5 %collective-permute-start.14 = (bf16[528,768]{1,0:T(8,128)(2,1)S(1)}, bf16[528,768]{1,0:T(8,128)(2,1)}, u32[]{:S(2)}, u32[]{:S(2)}) collective-permute-start(bf16[528,768]{1,0:T(8,128)(2,1)S(1)} %collective-permute-done.4.refs_3_.refs_6_), channel_id=1, source_target_pairs={{0,1},{1,0},{2,3},{3,2},{4,5},{5,4},{6,7},{7,6},{8,9},{9,8},{10,11... | collective-permute-start | bytes 2433032 | tf_op jit(solution)/shard_map/ppermute | solution.py:84
  28.6 0.7 copy-start.9
  28.6 0.7 copy-start.8
  29.4 0.7 copy-start.10
  30.6 15.9 %copy-start.7 = (pred[21]{0:T(512)(128)(4,1)S(1)}, pred[21]{0:T(512)(128)(4,1)}, u32[]{:S(2)}) copy-start(pred[21]{0:T(512)(128)(4,1)} %constant.127.clone) | copy-start | bytes 67
  33.5 23.9 %collective-permute-start.17 = (bf16[528,768]{1,0:T(8,128)(2,1)S(1)}, bf16[528,768]{1,0:T(8,128)(2,1)}, u32[]{:S(2)}, u32[]{:S(2)}) collective-permute-start(bf16[528,768]{1,0:T(8,128)(2,1)S(1)} %collective-permute-done.8.refs_2_.refs_5_.refs_3_), channel_id=1, source_target_pairs={{0,1},{1,0},{2,3},{3,2},{4,5},{5,4},{6,7},{7,6},{8,9},{9,8},{10,11... | collective-permute-start | bytes 2433032 | tf_op jit(solution)/shard_map/ppermute | solution.py:84
  33.5 26.8 %collective-permute-start.6 = (bf16[528,768]{1,0:T(8,128)(2,1)}, bf16[528,768]{1,0:T(8,128)(2,1)}, u32[]{:S(2)}, u32[]{:S(2)}) collective-permute-start(bf16[528,768]{1,0:T(8,128)(2,1)} %collective-permute-done.5.refs_2_.refs_9_), channel_id=1, source_target_pairs={{0,48},{1,17},{2,50},{3,19},{4,52},{5,21},{6,54},{7,23},{8,56},{9,... | collective-permute-start | bytes 2433032 | tf_op jit(solution)/shard_map/ppermute | solution.py:80
  34.5 27.2 %collective-permute-start.15 = (bf16[528,768]{1,0:T(8,128)(2,1)}, bf16[528,768]{1,0:T(8,128)(2,1)}, u32[]{:S(2)}, u32[]{:S(2)}) collective-permute-start(bf16[528,768]{1,0:T(8,128)(2,1)} %collective-permute-done.5.refs_2_.refs_9_), channel_id=1, source_target_pairs={{0,1},{1,0},{2,3},{3,2},{4,5},{5,4},{6,7},{7,6},{8,9},{9,8},{10,11... | collective-permute-start | bytes 2433032 | tf_op jit(solution)/shard_map/ppermute | solution.py:84
  46.0 14.3 %collective-permute-start.18 = (bf16[528,768]{1,0:T(8,128)(2,1)}, bf16[528,768]{1,0:T(8,128)(2,1)}, u32[]{:S(2)}, u32[]{:S(2)}) collective-permute-start(bf16[528,768]{1,0:T(8,128)(2,1)} %collective-permute-done.9.refs_0_.refs_7_), channel_id=1, source_target_pairs={{0,1},{1,0},{2,3},{3,2},{4,5},{5,4},{6,7},{7,6},{8,9},{9,8},{10,11... | collective-permute-start | bytes 2433032 | tf_op jit(solution)/shard_map/ppermute | solution.py:84
  46.0 17.1 %collective-permute-start.19 = (bf16[528,768]{1,0:T(8,128)(2,1)}, bf16[528,768]{1,0:T(8,128)(2,1)}, u32[]{:S(2)}, u32[]{:S(2)}) collective-permute-start(bf16[528,768]{1,0:T(8,128)(2,1)} %collective-permute-done.1.refs_1_.refs_8_), channel_id=1, source_target_pairs={{0,1},{1,0},{2,3},{3,2},{4,5},{5,4},{6,7},{7,6},{8,9},{9,8},{10,11... | collective-permute-start | bytes 2433032 | tf_op jit(solution)/shard_map/ppermute | solution.py:84
  46.8 0.7 copy-start.6
  47.5 1.1 copy-start
  48.6 14.5 %copy-start.5 = (s32[2,23]{1,0:T(2,128)S(1)}, s32[2,23]{1,0:T(2,128)}, u32[]{:S(2)}) copy-start(s32[2,23]{1,0:T(2,128)} %constant.121.clone.table) | copy-start | bytes 556
  57.3 23.6 %copy-start.4 = (s32[2,28]{1,0:T(2,128)S(1)}, s32[2,28]{1,0:T(2,128)}, u32[]{:S(2)}) copy-start(s32[2,28]{1,0:T(2,128)} %constant.122.clone.table) | copy-start | bytes 676
  57.4 20.6 %collective-permute-start.10 = (bf16[528,768]{1,0:T(8,128)(2,1)}, bf16[528,768]{1,0:T(8,128)(2,1)S(1)}, u32[]{:S(2)}, u32[]{:S(2)}) collective-permute-start(bf16[528,768]{1,0:T(8,128)(2,1)} %collective-permute-done.9.refs_0_.refs_7_), channel_id=1, source_target_pairs={{0,4},{1,3},{2,6},{3,65},{4,8},{5,7},{6,10},{7,69},{8,12},{9,11},{... | collective-permute-start | bytes 2433032 | tf_op jit(solution)/shard_map/ppermute | solution.py:80
  60.3 19.7 %collective-permute-start.11 = (bf16[528,768]{1,0:T(8,128)(2,1)}, bf16[528,768]{1,0:T(8,128)(2,1)S(1)}, u32[]{:S(2)}, u32[]{:S(2)}) collective-permute-start(bf16[528,768]{1,0:T(8,128)(2,1)} %collective-permute-done.9.refs_0_.refs_7_), channel_id=1, source_target_pairs={{0,66},{1,13},{2,0},{3,15},{4,70},{5,1},{6,4},{7,3},{8,74},{9,5},{... | collective-permute-start | bytes 2433032 | tf_op jit(solution)/shard_map/ppermute | solution.py:80
  60.3 38.5 %collective-permute-start.2 = (bf16[528,768]{1,0:T(8,128)(2,1)}, bf16[528,768]{1,0:T(8,128)(2,1)S(1)}, u32[]{:S(2)}, u32[]{:S(2)}) collective-permute-start(bf16[528,768]{1,0:T(8,128)(2,1)} %collective-permute-done.1.refs_1_.refs_8_), channel_id=1, source_target_pairs={{0,4},{1,3},{2,6},{3,65},{4,8},{5,7},{6,10},{7,69},{8,12},{9,11},{... | collective-permute-start | bytes 2433032 | tf_op jit(solution)/shard_map/ppermute | solution.py:80
  61.7 37.1 %collective-permute-start.3 = (bf16[528,768]{1,0:T(8,128)(2,1)}, bf16[528,768]{1,0:T(8,128)(2,1)S(1)}, u32[]{:S(2)}, u32[]{:S(2)}) collective-permute-start(bf16[528,768]{1,0:T(8,128)(2,1)} %collective-permute-done.1.refs_1_.refs_8_), channel_id=1, source_target_pairs={{0,12},{1,67},{2,14},{3,1},{4,0},{5,71},{6,2},{7,5},{8,4},{9,75},{... | collective-permute-start | bytes 2433032 | tf_op jit(solution)/shard_map/ppermute | solution.py:80
  63.1 17.0 %collective-permute-start.16 = (bf16[528,768]{1,0:T(8,128)(2,1)}, bf16[528,768]{1,0:T(8,128)(2,1)S(1)}, u32[]{:S(2)}, u32[]{:S(2)}) collective-permute-start(bf16[528,768]{1,0:T(8,128)(2,1)} %collective-permute-done.6.refs_0_), channel_id=1, source_target_pairs={{0,1},{1,0},{2,3},{3,2},{4,5},{5,4},{6,7},{7,6},{8,9},{9,8},{10,11... | collective-permute-start | bytes 2433032 | tf_op jit(solution)/shard_map/ppermute | solution.py:84
  78.0 20.9 %copy-start.3 = (s32[2,12]{1,0:T(2,128)S(1)}, s32[2,12]{1,0:T(2,128)}, u32[]{:S(2)}) copy-start(s32[2,12]{1,0:T(2,128)} %constant.128.clone.table) | copy-start | bytes 292
  78.0 20.9 %collective-permute-start.7 = (bf16[528,768]{1,0:T(8,128)(2,1)}, bf16[528,768]{1,0:T(8,128)(2,1)S(1)}, u32[]{:S(2)}, u32[]{:S(2)}) collective-permute-start(bf16[528,768]{1,0:T(8,128)(2,1)} %collective-permute-done.6.refs_0_), channel_id=1, source_target_pairs={{0,48},{1,17},{2,50},{3,19},{4,52},{5,21},{6,54},{7,23},{8,56},{9,... | collective-permute-start | bytes 2433032 | tf_op jit(solution)/shard_map/ppermute | solution.py:80
  80.0 0.9 copy-start.1
  98.9 1.1 copy-start.2

commit v4 on v3

--- a/solution.py
+++ b/solution.py
@@ -84,6 +84,21 @@
     return lax.ppermute(block, AXES, [(i, i ^ 1) for i in range(128)])
 
 
+def home(name, group, row):
+    x, y, z = lax.rem(group, 4), lax.div(group, 4) * 2 + lax.rem(lax.div(row, 2), 2), lax.div(row, 4)
+    core = lax.rem(row, 2)
+    table = offsets()
+    swap = 1 if name >= OTHER else 0
+    at = []
+    for axis, here in enumerate((x, y, z)):
+        first = table[swap][name % OTHER][axis]
+        second = table[1 - swap][name % OTHER][axis]
+        at.append(lax.rem(here + jnp.where(core == 0, first, second), 4))
+    core = 1 - core if swap else core
+    group = lax.div(at[1], 2) * 4 + at[0]
+    return group * 16 + (at[2] * 2 + lax.rem(at[1], 2)) * 2 + core
+
+
 def prepare_kernel(embeds_ref, member_ref, block_ref, target_ref):
     member = member_ref[...].astype(jnp.float32)
     column = jnp.transpose(jnp.broadcast_to(member, (128, RB)))[:, 0:1]
@@ -116,26 +131,25 @@
     )(embeds, member.reshape(1, RB))
 
 
-def meet_kernel(total, rows, pairs, itself, lists, table, *refs):
+def meet_kernel(total, rows, pairs, itself, lists, table, waits, *refs):
     blocks, refs = refs[:total], refs[total:]
     if lists:
-        where_ref, refs = refs[0], refs[1:]
+        place_ref, refs = refs[0], refs[1:]
         before, refs = refs[: len(lists) - 1], refs[len(lists) - 1 :]
     out_ref, held, across, down, row_best, column_best, sems = refs
-    copies = []
     for k in range(total):
-        copies.append(pltpu.make_async_copy(blocks[k], held.at[k], sems.at[k]))
-        copies[k].start()
+        pltpu.make_async_copy(blocks[k], held.at[k], sems.at[k]).start()
     row_best[...] = jnp.full_like(row_best, LOW)
     column_best[...] = jnp.full_like(column_best, LOW)
     if lists:
         out_ref[...] = jnp.full_like(out_ref, ABSENT)
-    for k in range(total):
-        copies[k].wait()
-        clusters = held[k, RB:SENT, 0:RB].astype(jnp.float32)[0:8]
-        across[k] = clusters
-        if k < rows:
-            down[k] = jnp.transpose(jnp.broadcast_to(clusters[0:1], (128, RB)))
+    def arrive(k):
+        pltpu.make_async_copy(blocks[0], held.at[k], sems.at[k]).wait()
+        across[k] = held[k, RB:SENT, 0:RB].astype(jnp.float32)[0:8]
+
+    for k in range(rows):
+        arrive(k)
+        down[k] = jnp.transpose(jnp.broadcast_to(across[k, 0:1], (128, RB)))
 
     def meet(i, j, same):
         scores = lax.dot_general(
@@ -159,14 +173,22 @@
     if itself:
         meet(0, 0, True)
 
+    def await_step(step, length):
+        for u in range(length):
+            block = waits[step * UNROLL + u]
+            pl.when(block >= 0)(functools.partial(arrive, block))
+
     def some(step, carry):
+        await_step(step, UNROLL)
         for u in range(UNROLL):
             p = step * UNROLL + u
             meet(table[0, p], table[1, p], False)
         return carry
 
-    lax.fori_loop(0, pairs // UNROLL, some, 0)
-    for p in range(pairs // UNROLL * UNROLL, pairs):
+    steps = pairs // UNROLL
+    lax.fori_loop(0, steps, some, 0)
+    await_step(steps, pairs - steps * UNROLL)
+    for p in range(steps * UNROLL, pairs):
         meet(table[0, p], table[1, p], False)
 
     def found_in(k):
@@ -188,17 +210,23 @@
             if name in names:
                 at = names.index(name)
                 found = jnp.maximum(found, ref[at : at + 1, :])
-        out_ref[where_ref[number]] = found
-
-
-def meet(held, meeting, lists=(), where=None, before=()):
+        out_ref[home(name, place_ref[0], place_ref[1])] = found
+
+
+def meet(held, meeting, lists=(), before=()):
     rows, names = members(meeting)
     pairs = [(i, j) for i, partners in meeting for j in partners]
     itself = (0, 0) in pairs
-    pairs = [(names.index(i), names.index(j)) for i, j in pairs if i != j]
+    pairs = sorted(
+        ((names.index(i), names.index(j)) for i, j in pairs if i != j), key=lambda p: p[::-1]
+    )
+    seen, waits = set(range(len(rows))), []
+    for i, j in pairs:
+        waits.append(-1 if j in seen else j)
+        seen.add(j)
     total = len(names)
     shape = (128, 1, RB) if lists else (total, RB)
-    in_specs = [pl.BlockSpec(memory_space=pltpu.SMEM)]
+    in_specs = [pl.BlockSpec(memory_space=pltpu.SMEM)] * 2
     in_specs += [pl.BlockSpec(memory_space=pl.ANY)] * total
     if lists:
         in_specs += [pl.BlockSpec(memory_space=pltpu.SMEM)]
@@ -215,7 +243,7 @@
             pltpu.VMEM((total, 8, RB), jnp.float32),
             pltpu.SemaphoreType.DMA((total,)),
         ],
-        compiler_params=pltpu.CompilerParams(vmem_limit_bytes=40 * 2**20),
+        compiler_params=pltpu.CompilerParams(vmem_limit_bytes=58 * 2**20),
         cost_estimate=pl.CostEstimate(
             flops=2 * RB * RB * D * len(pairs),
             bytes_accessed=total * SENT * D * 2,
@@ -224,14 +252,15 @@
         name=f"meet_{len(pairs)}",
     )(
         jnp.asarray(np.array(pairs, np.int32).T),
+        jnp.asarray(np.array(waits, np.int32)),
         *[held[k] for k in names],
-        *(() if where is None else (where,)),
+        *((jnp.stack([lax.axis_index(axis) for axis in AXES]),) if lists else ()),
         *before,
     )
 
 
 def finish_kernel(arrived_ref, target_ref, out_ref):
-    best = jnp.max(arrived_ref[...], axis=0, keepdims=True)
+    best = jnp.max(arrived_ref[...], axis=0)
     column = jnp.transpose(jnp.broadcast_to(best, (128, RB)))[:, 0:1]
     above = lax.broadcasted_iota(jnp.int32, (RB, RB), 0)
     picked = jnp.where(above == target_ref[...], column, LOW)
@@ -244,32 +273,41 @@
     )(arrived, target)
 
 
-def homes():
-    group, row = lax.axis_index("group"), lax.axis_index("row")
-    x, y, z, core = group % 4, (group // 4) * 2 + (row // 2) % 2, row // 4, row % 2
-    table = jnp.array(offsets(), jnp.int32)
-    own = jnp.where(core == 0, table[0], table[1])
-    other = jnp.where(core == 0, table[1], table[0])
-    names = np.array(NAMES)
-    steps = jnp.where((names < OTHER)[:, None], own[names % OTHER], other[names % OTHER])
-    cores = jnp.where(names < OTHER, core, 1 - core)
-    at = place((x + steps[:, 0]) % 4, (y + steps[:, 1]) % 4, (z + steps[:, 2]) % 4, cores)
-    return at.astype(jnp.int32)
-
-
 def on_device(embeds, member):
     block, target = prepare(embeds, member)
     held = {0: block}
-    for i in range(1, SLOTS):
-        held[i] = fetch(held[PARENT[i]], (UNIT[DIRS[0][i]], UNIT[DIRS[1][i]]))
-    for name in NAMES:
-        if name >= OTHER:
-            held[name] = flip(held[name - OTHER])
-    before = [meet(held, meeting) for meeting in MEETINGS[:-1]]
+    before = []
+
+    def go(first):
+        for i in range(first, first + 3):
+            held[i] = fetch(held[PARENT[i]], (UNIT[DIRS[0][i]], UNIT[DIRS[1][i]]))
+
+    def share(slots):
+        for i in slots:
+            if i + OTHER in NAMES:
+                held[i + OTHER] = flip(held[i])
+
+    def after(slots):
+        kept = lax.optimization_barrier((before[-1], *[held[i] for i in slots]))
+        before[-1] = kept[0]
+        held.update(zip(slots, kept[1:]))
+
+    go(1)
+    share((0, 1))
+    go(4)
+    before.append(meet(held, MEETINGS[0]))
+    after((2, 3, 4, 5, 6))
+    go(7)
+    share((2, 3, 4, 5, 6))
+    before.append(meet(held, MEETINGS[1]))
+    after((7, 8, 9))
+    go(10)
+    share((7, 8, 9))
+    before.append(meet(held, MEETINGS[2]))
     lists = tuple(members(meeting)[1] for meeting in (MEETINGS[-1],) + MEETINGS[:-1])
-    outgoing = meet(held, MEETINGS[-1], lists, homes(), before)
+    outgoing = meet(held, MEETINGS[-1], lists, before)
     arrived = lax.all_to_all(outgoing, AXES, split_axis=0, concat_axis=0, tiled=True)
-    return finish(arrived.reshape(128, RB), target).reshape(-1)
+    return finish(arrived, target).reshape(-1)
 
 
 def solution(mesh):

time: 128 us -> 117 us (0.914)
  starting transfers between devices: 36.9 us -> 24.7 us
  waiting for transfers between devices: 11.7 us -> 8.41 us
  blocking collectives: 16.7 us -> 18.4 us
    ppermute x8, starting transfers between devices: 19.6 us -> 9.46 us  [flip(): return lax.ppermute(block, AXES, [(i, i ^ 1) for i in range(128)])]
    ppermute x12, waiting for transfers between devices: 11.7 us -> 6.16 us  [fetch(): return lax.ppermute(block, AXES, sorted(pairs))]
    ppermute x8, waiting for transfers between devices: 0.02 us -> 2.26 us  [flip(): return lax.ppermute(block, AXES, [(i, i ^ 1) for i in range(128)])]
    ppermute x12, starting transfers between devices: 17.3 us -> 15.2 us  [fetch(): return lax.ppermute(block, AXES, sorted(pairs))]
    unnamed x23 -> x34, local copies, waits for them, and re-layouts: 5.81 us -> 7.83 us
    all_to_all x1, blocking collectives: 16.7 us -> 18.4 us  [on_device(): lax.all_to_all(outgoing, AXES, split_axis=0, concat_axis=0, tiled=True)]
  transfers between devices with their start and end apart: 20 -> 20, of which waited for: 5 -> 4; matrix products, arithmetic and copies ran while one was open for 1% -> 1% of each run, Pallas kernels for 32% -> 35%
where the time goes in v4:
time: 117 us; the launch traced here: 116 us
  Pallas kernels  56.1 us (48%)
  starting transfers between devices  24.7 us (21%)
  blocking collectives  18.4 us (16%)
  waiting for transfers between devices  8.41 us (7%)
  local copies, waits for them, and re-layouts  7.83 us (7%)
    pallas_call x4, Pallas kernels, meet(): pl.pallas_call(functools.partial(meet_kernel, total, len(rows), len(pairs...  51.1 us
    all_to_all x1, blocking collectives, on_device(): lax.all_to_all(outgoing, AXES, split_axis=0, concat_axis=0, tiled=True)  18.4 us
    ppermute x12, starting transfers between devices, fetch(): return lax.ppermute(block, AXES, sorted(pairs))  15.2 us
    ppermute x8, starting transfers between devices, flip(): return lax.ppermute(block, AXES, [(i, i ^ 1) for i in range(128)])  9.46 us
    unnamed x34, local copies, waits for them, and re-layouts  7.83 us
    ppermute x12, waiting for transfers between devices, fetch(): return lax.ppermute(block, AXES, sorted(pairs))  6.16 us
    pallas_call x1, Pallas kernels, prepare(): pl.pallas_call(prepare_kernel, out_shape=(jax.ShapeDtypeStruct((SENT, D),...  3.11 us
  transfers between devices with their start and end apart: 20, of which 4 were waited for; matrix products, arithmetic and copies ran while one was open for 1% of the time, Pallas kernels for 35%

profile of v4, /device:TPU:1, one launch (start us, length us, event | category | flops | bytes accessed | tf_op | source)
XLA Modules:
  0.0 116.3 jit_solution(11644649810631382074)
XLA Ops:
  0.0 3.1 %prepare.1 = (bf16[528,768]{1,0:T(8,128)(2,1)}, s32[1,512]{1,0:T(1,128)}) custom-call(bf16[512,768]{1,0:T(8,128)(2,1)} %embeds_ref.1, s32[1,512]{1,0:T(1,128)} %bitcast.4), custom_call_target="tpu_custom_call" | custom-call | tf_op jit(solution)/shard_map/prepare/pallas_call | solution.py:124
  3.1 2.1 %collective-permute-start = (bf16[528,768]{1,0:T(8,128)(2,1)}, bf16[528,768]{1,0:T(8,128)(2,1)S(1)}, u32[]{:S(2)}, u32[]{:S(2)}) collective-permute-start(bf16[528,768]{1,0:T(8,128)(2,1)} %get-tuple-element.17.refs_0_.refs_3_), channel_id=1, source_target_pairs={{0,4},{1,3},{2,6},{3,65},{4,8},{5,7},{6,10},{7,69},{8,12},{9,11},{... | collective-permute-start | bytes 2433032 | tf_op jit(solution)/shard_map/ppermute | solution.py:80
  5.2 1.2 %collective-permute-start.1 = (bf16[528,768]{1,0:T(8,128)(2,1)}, bf16[528,768]{1,0:T(8,128)(2,1)S(1)}, u32[]{:S(2)}, u32[]{:S(2)}) collective-permute-start(bf16[528,768]{1,0:T(8,128)(2,1)} %get-tuple-element.17.refs_0_.refs_3_), channel_id=1, source_target_pairs={{0,48},{1,17},{2,50},{3,19},{4,52},{5,21},{6,54},{7,23},{8,56},{9,... | collective-permute-start | bytes 2433032 | tf_op jit(solution)/shard_map/ppermute | solution.py:80
  6.4 1.4 %collective-permute-start.2 = (bf16[528,768]{1,0:T(8,128)(2,1)}, bf16[528,768]{1,0:T(8,128)(2,1)S(1)}, u32[]{:S(2)}, u32[]{:S(2)}) collective-permute-start(bf16[528,768]{1,0:T(8,128)(2,1)} %get-tuple-element.17.refs_0_.refs_3_), channel_id=1, source_target_pairs={{0,12},{1,67},{2,14},{3,1},{4,0},{5,71},{6,2},{7,5},{8,4},{9,75},{... | collective-permute-start | bytes 2433032 | tf_op jit(solution)/shard_map/ppermute | solution.py:80
  7.9 3.5 %collective-permute-start.3 = (bf16[528,768]{1,0:T(8,128)(2,1)}, bf16[528,768]{1,0:T(8,128)(2,1)S(1)}, u32[]{:S(2)}, u32[]{:S(2)}) collective-permute-start(bf16[528,768]{1,0:T(8,128)(2,1)} %get-tuple-element.17.refs_0_.refs_3_), channel_id=1, source_target_pairs={{0,1},{1,0},{2,3},{3,2},{4,5},{5,4},{6,7},{7,6},{8,9},{9,8},{10,11... | collective-permute-start | bytes 2433032 | tf_op jit(solution)/shard_map/ppermute | solution.py:84
  11.4 5.4 %collective-permute-done.refs_1_.refs_4_ = bf16[528,768]{1,0:T(8,128)(2,1)S(1)} collective-permute-done((bf16[528,768]{1,0:T(8,128)(2,1)}, bf16[528,768]{1,0:T(8,128)(2,1)S(1)}, u32[]{:S(2)}, u32[]{:S(2)}) %collective-permute-start) | collective-permute-done | bytes 811040 | tf_op jit(solution)/shard_map/ppermute | solution.py:80
  16.8 2.3 %collective-permute-start.4 = (bf16[528,768]{1,0:T(8,128)(2,1)S(1)}, bf16[528,768]{1,0:T(8,128)(2,1)S(1)}, u32[]{:S(2)}, u32[]{:S(2)}) collective-permute-start(bf16[528,768]{1,0:T(8,128)(2,1)S(1)} %collective-permute-done.refs_1_.refs_4_), channel_id=1, source_target_pairs={{0,1},{1,0},{2,3},{3,2},{4,5},{5,4},{6,7},{7,6},{8,9},{9,8},{10,11... | collective-permute-start | bytes 2433032 | tf_op jit(solution)/shard_map/ppermute | solution.py:84
  19.1 2.5 %collective-permute-start.6 = (bf16[528,768]{1,0:T(8,128)(2,1)S(1)}, bf16[528,768]{1,0:T(8,128)(2,1)S(1)}, u32[]{:S(2)}, u32[]{:S(2)}) collective-permute-start(bf16[528,768]{1,0:T(8,128)(2,1)S(1)} %collective-permute-done.refs_1_.refs_4_), channel_id=1, source_target_pairs={{0,16},{1,49},{2,18},{3,51},{4,20},{5,53},{6,22},{7,55},{8,24},{9,... | collective-permute-start | bytes 2433032 | tf_op jit(solution)/shard_map/ppermute | solution.py:80
  21.6 0.0 collective-permute-done.1.refs_2_.refs_5_.refs_3_
  21.6 1.7 %collective-permute-start.5 = (bf16[528,768]{1,0:T(8,128)(2,1)S(1)}, bf16[528,768]{1,0:T(8,128)(2,1)S(1)}, u32[]{:S(2)}, u32[]{:S(2)}) collective-permute-start(bf16[528,768]{1,0:T(8,128)(2,1)S(1)} %collective-permute-done.1.refs_2_.refs_5_.refs_3_), channel_id=1, source_target_pairs={{0,66},{1,13},{2,0},{3,15},{4,70},{5,1},{6,4},{7,3},{8,74},{9,5},{... | collective-permute-start | bytes 2433032 | tf_op jit(solution)/shard_map/ppermute | solution.py:80
  23.3 0.0 collective-permute-done.2.refs_3_.refs_6_
  23.3 0.0 collective-permute-start.7
  23.3 0.0 collective-permute-done.3.refs_4_.refs_7_.refs_10_.refs_6_
  23.3 0.0 copy-start.1
  23.4 0.0 collective-permute-done.4.refs_5_.refs_8_.refs_11_.refs_7_
  23.4 0.8 copy-done.4
  24.2 0.3 copy-done.1
  24.5 0.9 copy-done.2
  25.4 9.9 %meet_12.2.refs_12_ = f32[6,512]{1,0:T(8,128)} custom-call(s32[2,12]{1,0:T(2,128)} %constant.25.clone.table, s32[12]{0:T(128)} %constant.26.clone.waits, bf16[528,768]{1,0:T(8,128)(2,1)} %get-tuple-element.17.refs_0_.refs_3_, bf16[528,768]{1,0:T(8,128)(2,1)} %copy-done.3, bf16[528,768]{1,0:T(8,128)(2,1)} %copy-done, bf16[528,768]{1,0:T(8,128)(2,1)} %copy-done.4, ...), custom_call_target="tpu_custom_call" | custom-call | flops 4831838208 | bytes 4866048 | tf_op jit(solution)/shard_map/meet_12/pallas_call | solution.py:234
  35.3 0.0 collective-permute-done.6.refs_1_.refs_8_
  35.3 0.0 collective-permute-done.5.refs_0_.refs_7_
  35.3 0.7 collective-permute-done.7.refs_2_.refs_9_
  36.0 1.1 collective-permute-start.10
  37.2 0.0 collective-permute-start.11
  37.2 0.5 collective-permute-start.12
  37.7 0.0 collective-permute-start.13
  37.7 0.5 collective-permute-start.14
  38.2 1.1 collective-permute-done.10.refs_9_.refs_12_
  39.3 1.2 %collective-permute-start.15 = (bf16[528,768]{1,0:T(8,128)(2,1)}, bf16[528,768]{1,0:T(8,128)(2,1)}, u32[]{:S(2)}, u32[]{:S(2)}) collective-permute-start(bf16[528,768]{1,0:T(8,128)(2,1)} %collective-permute-done.7.refs_2_.refs_9_), channel_id=1, source_target_pairs={{0,48},{1,17},{2,50},{3,19},{4,52},{5,21},{6,54},{7,23},{8,56},{9,... | collective-permute-start | bytes 2433032 | tf_op jit(solution)/shard_map/ppermute | solution.py:80
  40.6 1.1 collective-permute-done.11.refs_10_.refs_13_.refs_8_
  41.7 0.2 collective-permute-start.16
  41.9 0.0 collective-permute-done.12.refs_11_.refs_14_
  41.9 2.1 %collective-permute-start.17 = (bf16[528,768]{1,0:T(8,128)(2,1)S(1)}, bf16[528,768]{1,0:T(8,128)(2,1)}, u32[]{:S(2)}, u32[]{:S(2)}) collective-permute-start(bf16[528,768]{1,0:T(8,128)(2,1)S(1)} %collective-permute-done.5.refs_0_.refs_7_), channel_id=1, source_target_pairs={{0,66},{1,13},{2,0},{3,15},{4,70},{5,1},{6,4},{7,3},{8,74},{9,5},{... | collective-permute-start | bytes 2433032 | tf_op jit(solution)/shard_map/ppermute | solution.py:80
  44.0 0.0 collective-permute-done.13.refs_12_.refs_15_
  44.0 0.9 copy-done.12
  44.9 0.0 collective-permute-done.14.refs_13_.refs_16_.refs_9_
  44.9 0.0 copy-done.6
  44.9 0.0 copy-done.9
  44.9 0.0 copy-done.7
  44.9 0.0 copy-done.10
  44.9 0.0 copy-start.8
  45.0 0.9 copy-done.8
  45.9 14.5 %meet_23.1.refs_13_ = f32[14,512]{1,0:T(8,128)} custom-call(s32[2,23]{1,0:T(2,128)} %constant.27.clone.table, s32[23]{0:T(128)} %constant.28.clone.waits, bf16[528,768]{1,0:T(8,128)(2,1)} %copy-done.6, bf16[528,768]{1,0:T(8,128)(2,1)} %copy-done.5, bf16[528,768]{1,0:T(8,128)(2,1)} %collective-permute-done.7.refs_2_.refs_9_, ...), custom_call_target="tpu_custom_call" | custom-call | flops 9261023232 | bytes 11354112 | tf_op jit(solution)/shard_map/meet_23/pallas_call | solution.py:234
  60.3 0.0 collective-permute-done.15.refs_0_
  60.4 0.0 collective-permute-done.16.refs_1_.refs_4_
  60.4 0.0 collective-permute-done.17.refs_2_.refs_5_
  60.4 0.9 copy-done.11
  61.3 1.5 %collective-permute-start.19 = (bf16[528,768]{1,0:T(8,128)(2,1)}, bf16[528,768]{1,0:T(8,128)(2,1)S(1)}, u32[]{:S(2)}, u32[]{:S(2)}) collective-permute-start(bf16[528,768]{1,0:T(8,128)(2,1)} %collective-permute-done.15.refs_0_), channel_id=1, source_target_pairs={{0,1},{1,0},{2,3},{3,2},{4,5},{5,4},{6,7},{7,6},{8,9},{9,8},{10,11... | collective-permute-start | bytes 2433032 | tf_op jit(solution)/shard_map/ppermute | solution.py:84
  62.8 0.6 pad_add_fusion.refs_11_
  63.4 0.3 collective-permute-start.8
  63.7 2.4 %collective-permute-start.9 = (bf16[528,768]{1,0:T(8,128)(2,1)}, bf16[528,768]{1,0:T(8,128)(2,1)S(1)}, u32[]{:S(2)}, u32[]{:S(2)}) collective-permute-start(bf16[528,768]{1,0:T(8,128)(2,1)} %copy-done.5), channel_id=1, source_target_pairs={{0,12},{1,67},{2,14},{3,1},{4,0},{5,71},{6,2},{7,5},{8,4},{9,75},{... | collective-permute-start | bytes 2433032 | tf_op jit(solution)/shard_map/ppermute | solution.py:80
  66.1 0.0 collective-permute-start.18
  66.1 0.0 collective-permute-done.19.refs_17_.refs_10_
  66.1 0.9 copy-done.13
  67.0 16.8 %meet_28.1.refs_14_ = f32[18,512]{1,0:T(8,128)} custom-call(s32[2,28]{1,0:T(2,128)} %constant.29.clone.table, s32[28]{0:T(128)} %constant.30.clone.waits, bf16[528,768]{1,0:T(8,128)(2,1)} %collective-permute-done.15.refs_0_, bf16[528,768]{1,0:T(8,128)(2,1)} %copy-done.11, bf16[528,768]{1,0:T(8,128)(2,1)} %collective-permute-done.17.refs_2_.refs_5_, ...), custom_call_target="tpu_custom_call" | custom-call | flops 11274289152 | bytes 14598144 | tf_op jit(solution)/shard_map/meet_28/pallas_call | solution.py:234
  83.8 0.0 collective-permute-done.8.refs_0_
  83.8 0.0 collective-permute-done.9.refs_1_
  83.8 0.0 collective-permute-done.18.refs_2_
  83.8 0.8 copy-done.14
  84.7 0.3 copy-done.15
  85.0 1.0 copy-done.16
  86.0 10.0 %meet_12.3 = f32[128,1,512]{2,1,0:T(1,128)} custom-call(s32[2,12]{1,0:T(2,128)} %constant.31.clone.table, s32[12]{0:T(128)} %constant.32.clone.waits, bf16[528,768]{1,0:T(8,128)(2,1)} %copy-done.14, bf16[528,768]{1,0:T(8,128)(2,1)} %copy-done.15, bf16[528,768]{1,0:T(8,128)(2,1)} %copy-done.16, bf16[528,768]{1,0:T(8,128)(2,1)} %copy-done, ...), custom_call_target="tpu_custom_call" | custom-call | flops 4831838208 | bytes 8921088 | tf_op jit(solution)/shard_map/meet_12/pallas_call | solution.py:234
  96.0 18.4 %all_to_all.5.arrived_ref = f32[128,1,512]{2,1,0:T(1,128)} all-to-all(f32[128,1,512]{2,1,0:T(1,128)} %meet_12.3), channel_id=1, replica_groups=mesh['group'=8,'row'=16] {'group','row'}, dimensions={0} | all-to-all | bytes 524288 | tf_op jit(solution)/shard_map/all_to_all | solution.py:309
  114.4 1.9 %finish.1 = f32[1,512]{1,0:T(1,128)} custom-call(f32[128,1,512]{2,1,0:T(1,128)} %all_to_all.5.arrived_ref, s32[1,512]{1,0:T(1,128)} %get-tuple-element.28.target_ref), custom_call_target="tpu_custom_call" | custom-call | tf_op jit(solution)/shard_map/finish/pallas_call | solution.py:271
  (18 shorter events, 0.0 us)
Async XLA Ops:
  3.1 13.7 %collective-permute-start = (bf16[528,768]{1,0:T(8,128)(2,1)}, bf16[528,768]{1,0:T(8,128)(2,1)S(1)}, u32[]{:S(2)}, u32[]{:S(2)}) collective-permute-start(bf16[528,768]{1,0:T(8,128)(2,1)} %get-tuple-element.17.refs_0_.refs_3_), channel_id=1, source_target_pairs={{0,4},{1,3},{2,6},{3,65},{4,8},{5,7},{6,10},{7,69},{8,12},{9,11},{... | collective-permute-start | bytes 2433032 | tf_op jit(solution)/shard_map/ppermute | solution.py:80
  5.2 16.3 %collective-permute-start.1 = (bf16[528,768]{1,0:T(8,128)(2,1)}, bf16[528,768]{1,0:T(8,128)(2,1)S(1)}, u32[]{:S(2)}, u32[]{:S(2)}) collective-permute-start(bf16[528,768]{1,0:T(8,128)(2,1)} %get-tuple-element.17.refs_0_.refs_3_), channel_id=1, source_target_pairs={{0,48},{1,17},{2,50},{3,19},{4,52},{5,21},{6,54},{7,23},{8,56},{9,... | collective-permute-start | bytes 2433032 | tf_op jit(solution)/shard_map/ppermute | solution.py:80
  6.4 16.9 %collective-permute-start.2 = (bf16[528,768]{1,0:T(8,128)(2,1)}, bf16[528,768]{1,0:T(8,128)(2,1)S(1)}, u32[]{:S(2)}, u32[]{:S(2)}) collective-permute-start(bf16[528,768]{1,0:T(8,128)(2,1)} %get-tuple-element.17.refs_0_.refs_3_), channel_id=1, source_target_pairs={{0,12},{1,67},{2,14},{3,1},{4,0},{5,71},{6,2},{7,5},{8,4},{9,75},{... | collective-permute-start | bytes 2433032 | tf_op jit(solution)/shard_map/ppermute | solution.py:80
  7.9 15.4 %collective-permute-start.3 = (bf16[528,768]{1,0:T(8,128)(2,1)}, bf16[528,768]{1,0:T(8,128)(2,1)S(1)}, u32[]{:S(2)}, u32[]{:S(2)}) collective-permute-start(bf16[528,768]{1,0:T(8,128)(2,1)} %get-tuple-element.17.refs_0_.refs_3_), channel_id=1, source_target_pairs={{0,1},{1,0},{2,3},{3,2},{4,5},{5,4},{6,7},{7,6},{8,9},{9,8},{10,11... | collective-permute-start | bytes 2433032 | tf_op jit(solution)/shard_map/ppermute | solution.py:84
  16.8 6.5 %copy-start.3 = (bf16[528,768]{1,0:T(8,128)(2,1)}, bf16[528,768]{1,0:T(8,128)(2,1)S(1)}, u32[]{:S(2)}) copy-start(bf16[528,768]{1,0:T(8,128)(2,1)S(1)} %collective-permute-done.refs_1_.refs_4_) | copy-start | bytes 2433028
  16.8 6.5 %collective-permute-start.4 = (bf16[528,768]{1,0:T(8,128)(2,1)S(1)}, bf16[528,768]{1,0:T(8,128)(2,1)S(1)}, u32[]{:S(2)}, u32[]{:S(2)}) collective-permute-start(bf16[528,768]{1,0:T(8,128)(2,1)S(1)} %collective-permute-done.refs_1_.refs_4_), channel_id=1, source_target_pairs={{0,1},{1,0},{2,3},{3,2},{4,5},{5,4},{6,7},{7,6},{8,9},{9,8},{10,11... | collective-permute-start | bytes 2433032 | tf_op jit(solution)/shard_map/ppermute | solution.py:84
  19.1 16.2 %collective-permute-start.6 = (bf16[528,768]{1,0:T(8,128)(2,1)S(1)}, bf16[528,768]{1,0:T(8,128)(2,1)S(1)}, u32[]{:S(2)}, u32[]{:S(2)}) collective-permute-start(bf16[528,768]{1,0:T(8,128)(2,1)S(1)} %collective-permute-done.refs_1_.refs_4_), channel_id=1, source_target_pairs={{0,16},{1,49},{2,18},{3,51},{4,20},{5,53},{6,22},{7,55},{8,24},{9,... | collective-permute-start | bytes 2433032 | tf_op jit(solution)/shard_map/ppermute | solution.py:80
  21.6 1.8 %copy-start = (bf16[528,768]{1,0:T(8,128)(2,1)}, bf16[528,768]{1,0:T(8,128)(2,1)S(1)}, u32[]{:S(2)}) copy-start(bf16[528,768]{1,0:T(8,128)(2,1)S(1)} %collective-permute-done.1.refs_2_.refs_5_.refs_3_) | copy-start | bytes 2433028
  21.6 13.7 %collective-permute-start.5 = (bf16[528,768]{1,0:T(8,128)(2,1)S(1)}, bf16[528,768]{1,0:T(8,128)(2,1)S(1)}, u32[]{:S(2)}, u32[]{:S(2)}) collective-permute-start(bf16[528,768]{1,0:T(8,128)(2,1)S(1)} %collective-permute-done.1.refs_2_.refs_5_.refs_3_), channel_id=1, source_target_pairs={{0,66},{1,13},{2,0},{3,15},{4,70},{5,1},{6,4},{7,3},{8,74},{9,5},{... | collective-permute-start | bytes 2433032 | tf_op jit(solution)/shard_map/ppermute | solution.py:80
  23.3 0.9 copy-start.4
  23.3 12.7 %collective-permute-start.7 = (bf16[528,768]{1,0:T(8,128)(2,1)S(1)}, bf16[528,768]{1,0:T(8,128)(2,1)}, u32[]{:S(2)}, u32[]{:S(2)}) collective-permute-start(bf16[528,768]{1,0:T(8,128)(2,1)S(1)} %collective-permute-done.2.refs_3_.refs_6_), channel_id=1, source_target_pairs={{0,2},{1,5},{2,64},{3,7},{4,6},{5,9},{6,68},{7,11},{8,10},{9,13},{... | collective-permute-start | bytes 2433032 | tf_op jit(solution)/shard_map/ppermute | solution.py:80
  23.3 1.2 copy-start.1
  24.5 0.9 copy-start.2
  35.3 9.6 %copy-start.5 = (bf16[528,768]{1,0:T(8,128)(2,1)}, bf16[528,768]{1,0:T(8,128)(2,1)S(1)}, u32[]{:S(2)}) copy-start(bf16[528,768]{1,0:T(8,128)(2,1)S(1)} %collective-permute-done.6.refs_1_.refs_8_) | copy-start | bytes 2433028
  35.3 9.6 %copy-start.6 = (bf16[528,768]{1,0:T(8,128)(2,1)}, bf16[528,768]{1,0:T(8,128)(2,1)S(1)}, u32[]{:S(2)}) copy-start(bf16[528,768]{1,0:T(8,128)(2,1)S(1)} %collective-permute-done.5.refs_0_.refs_7_) | copy-start | bytes 2433028
  36.0 3.3 %collective-permute-start.10 = (bf16[528,768]{1,0:T(8,128)(2,1)}, bf16[528,768]{1,0:T(8,128)(2,1)S(1)}, u32[]{:S(2)}, u32[]{:S(2)}) collective-permute-start(bf16[528,768]{1,0:T(8,128)(2,1)} %copy-done), channel_id=1, source_target_pairs={{0,1},{1,0},{2,3},{3,2},{4,5},{5,4},{6,7},{7,6},{8,9},{9,8},{10,11... | collective-permute-start | bytes 2433032 | tf_op jit(solution)/shard_map/ppermute | solution.py:84
  37.2 4.5 %collective-permute-start.11 = (bf16[528,768]{1,0:T(8,128)(2,1)}, bf16[528,768]{1,0:T(8,128)(2,1)S(1)}, u32[]{:S(2)}, u32[]{:S(2)}) collective-permute-start(bf16[528,768]{1,0:T(8,128)(2,1)} %copy-done.4), channel_id=1, source_target_pairs={{0,1},{1,0},{2,3},{3,2},{4,5},{5,4},{6,7},{7,6},{8,9},{9,8},{10,11... | collective-permute-start | bytes 2433032 | tf_op jit(solution)/shard_map/ppermute | solution.py:84
  37.2 4.7 %collective-permute-start.12 = (bf16[528,768]{1,0:T(8,128)(2,1)S(1)}, bf16[528,768]{1,0:T(8,128)(2,1)S(1)}, u32[]{:S(2)}, u32[]{:S(2)}) collective-permute-start(bf16[528,768]{1,0:T(8,128)(2,1)S(1)} %collective-permute-done.5.refs_0_.refs_7_), channel_id=1, source_target_pairs={{0,1},{1,0},{2,3},{3,2},{4,5},{5,4},{6,7},{7,6},{8,9},{9,8},{10,11... | collective-permute-start | bytes 2433032 | tf_op jit(solution)/shard_map/ppermute | solution.py:84
  37.7 6.3 %collective-permute-start.13 = (bf16[528,768]{1,0:T(8,128)(2,1)S(1)}, bf16[528,768]{1,0:T(8,128)(2,1)S(1)}, u32[]{:S(2)}, u32[]{:S(2)}) collective-permute-start(bf16[528,768]{1,0:T(8,128)(2,1)S(1)} %collective-permute-done.6.refs_1_.refs_8_), channel_id=1, source_target_pairs={{0,1},{1,0},{2,3},{3,2},{4,5},{5,4},{6,7},{7,6},{8,9},{9,8},{10,11... | collective-permute-start | bytes 2433032 | tf_op jit(solution)/shard_map/ppermute | solution.py:84
  37.7 7.2 %collective-permute-start.14 = (bf16[528,768]{1,0:T(8,128)(2,1)}, bf16[528,768]{1,0:T(8,128)(2,1)S(1)}, u32[]{:S(2)}, u32[]{:S(2)}) collective-permute-start(bf16[528,768]{1,0:T(8,128)(2,1)} %collective-permute-done.7.refs_2_.refs_9_), channel_id=1, source_target_pairs={{0,1},{1,0},{2,3},{3,2},{4,5},{5,4},{6,7},{7,6},{8,9},{9,8},{10,11... | collective-permute-start | bytes 2433032 | tf_op jit(solution)/shard_map/ppermute | solution.py:84
  39.3 5.6 %copy-start.9 = (bf16[528,768]{1,0:T(8,128)(2,1)}, bf16[528,768]{1,0:T(8,128)(2,1)S(1)}, u32[]{:S(2)}) copy-start(bf16[528,768]{1,0:T(8,128)(2,1)S(1)} %collective-permute-done.10.refs_9_.refs_12_) | copy-start | bytes 2433028
  39.3 21.0 %collective-permute-start.15 = (bf16[528,768]{1,0:T(8,128)(2,1)}, bf16[528,768]{1,0:T(8,128)(2,1)}, u32[]{:S(2)}, u32[]{:S(2)}) collective-permute-start(bf16[528,768]{1,0:T(8,128)(2,1)} %collective-permute-done.7.refs_2_.refs_9_), channel_id=1, source_target_pairs={{0,48},{1,17},{2,50},{3,19},{4,52},{5,21},{6,54},{7,23},{8,56},{9,... | collective-permute-start | bytes 2433032 | tf_op jit(solution)/shard_map/ppermute | solution.py:80
  41.7 3.3 %copy-start.7 = (bf16[528,768]{1,0:T(8,128)(2,1)}, bf16[528,768]{1,0:T(8,128)(2,1)S(1)}, u32[]{:S(2)}) copy-start(bf16[528,768]{1,0:T(8,128)(2,1)S(1)} %collective-permute-done.11.refs_10_.refs_13_.refs_8_) | copy-start | bytes 2433028
  41.7 18.7 %collective-permute-start.16 = (bf16[528,768]{1,0:T(8,128)(2,1)S(1)}, bf16[528,768]{1,0:T(8,128)(2,1)S(1)}, u32[]{:S(2)}, u32[]{:S(2)}) collective-permute-start(bf16[528,768]{1,0:T(8,128)(2,1)S(1)} %collective-permute-done.5.refs_0_.refs_7_), channel_id=1, source_target_pairs={{0,4},{1,3},{2,6},{3,65},{4,8},{5,7},{6,10},{7,69},{8,12},{9,11},{... | collective-permute-start | bytes 2433032 | tf_op jit(solution)/shard_map/ppermute | solution.py:80
  41.9 3.0 %copy-start.10 = (bf16[528,768]{1,0:T(8,128)(2,1)}, bf16[528,768]{1,0:T(8,128)(2,1)S(1)}, u32[]{:S(2)}) copy-start(bf16[528,768]{1,0:T(8,128)(2,1)S(1)} %collective-permute-done.12.refs_11_.refs_14_) | copy-start | bytes 2433028
  41.9 18.5 %collective-permute-start.17 = (bf16[528,768]{1,0:T(8,128)(2,1)S(1)}, bf16[528,768]{1,0:T(8,128)(2,1)}, u32[]{:S(2)}, u32[]{:S(2)}) collective-permute-start(bf16[528,768]{1,0:T(8,128)(2,1)S(1)} %collective-permute-done.5.refs_0_.refs_7_), channel_id=1, source_target_pairs={{0,66},{1,13},{2,0},{3,15},{4,70},{5,1},{6,4},{7,3},{8,74},{9,5},{... | collective-permute-start | bytes 2433032 | tf_op jit(solution)/shard_map/ppermute | solution.py:80
  44.0 0.9 copy-start.12
  44.9 0.9 copy-start.8
  60.4 0.9 copy-start.11
  61.3 4.8 %collective-permute-start.19 = (bf16[528,768]{1,0:T(8,128)(2,1)}, bf16[528,768]{1,0:T(8,128)(2,1)S(1)}, u32[]{:S(2)}, u32[]{:S(2)}) collective-permute-start(bf16[528,768]{1,0:T(8,128)(2,1)} %collective-permute-done.15.refs_0_), channel_id=1, source_target_pairs={{0,1},{1,0},{2,3},{3,2},{4,5},{5,4},{6,7},{7,6},{8,9},{9,8},{10,11... | collective-permute-start | bytes 2433032 | tf_op jit(solution)/shard_map/ppermute | solution.py:84
  63.4 20.4 %collective-permute-start.8 = (bf16[528,768]{1,0:T(8,128)(2,1)}, bf16[528,768]{1,0:T(8,128)(2,1)S(1)}, u32[]{:S(2)}, u32[]{:S(2)}) collective-permute-start(bf16[528,768]{1,0:T(8,128)(2,1)} %copy-done.5), channel_id=1, source_target_pairs={{0,4},{1,3},{2,6},{3,65},{4,8},{5,7},{6,10},{7,69},{8,12},{9,11},{... | collective-permute-start | bytes 2433032 | tf_op jit(solution)/shard_map/ppermute | solution.py:80
  63.7 20.2 %collective-permute-start.9 = (bf16[528,768]{1,0:T(8,128)(2,1)}, bf16[528,768]{1,0:T(8,128)(2,1)S(1)}, u32[]{:S(2)}, u32[]{:S(2)}) collective-permute-start(bf16[528,768]{1,0:T(8,128)(2,1)} %copy-done.5), channel_id=1, source_target_pairs={{0,12},{1,67},{2,14},{3,1},{4,0},{5,71},{6,2},{7,5},{8,4},{9,75},{... | collective-permute-start | bytes 2433032 | tf_op jit(solution)/shard_map/ppermute | solution.py:80
  66.1 17.8 %collective-permute-start.18 = (bf16[528,768]{1,0:T(8,128)(2,1)}, bf16[528,768]{1,0:T(8,128)(2,1)S(1)}, u32[]{:S(2)}, u32[]{:S(2)}) collective-permute-start(bf16[528,768]{1,0:T(8,128)(2,1)} %collective-permute-done.15.refs_0_), channel_id=1, source_target_pairs={{0,48},{1,17},{2,50},{3,19},{4,52},{5,21},{6,54},{7,23},{8,56},{9,... | collective-permute-start | bytes 2433032 | tf_op jit(solution)/shard_map/ppermute | solution.py:80
  66.1 0.9 copy-start.13
  83.8 0.9 copy-start.14
  83.8 1.2 %copy-start.15 = (bf16[528,768]{1,0:T(8,128)(2,1)}, bf16[528,768]{1,0:T(8,128)(2,1)S(1)}, u32[]{:S(2)}) copy-start(bf16[528,768]{1,0:T(8,128)(2,1)S(1)} %collective-permute-done.9.refs_1_) | copy-start | bytes 2433028
  85.0 1.0 copy-start.16
